TPU v7x, 32 devices: a whole 2x2x4 slice. The times are simulated.
32 devices in a mesh: grp: 2 (over x), tx: 16 (over z, y, core).
Axes of the slice: x: 2, y: 2, z: 4, core: 2. Of those that a mesh axis runs over, the one named last changes fastest.
Arguments:
- adjoint_in: float32 [3, 256, 256, 128], P(None, ('grp', 'tx')), parts along dimension 1, may hold values from -6 to 6
- forward_terms: bfloat16 [3, 3, 256, 256, 128], P(None, None, ('grp', 'tx')), parts along dimension 2, may hold values from -24 to 24
- log_conductivity: float32 [256, 256, 128], P(('grp', 'tx')), parts along dimension 0, may hold values from -1 to 1
- spacing: float32 [256, 256], P(('grp', 'tx')), parts along dimension 0, may hold values from 0.8 to 1.6
- residuals: float32 [35, 256, 256], P(None, ('grp', 'tx')), parts along dimension 1, may hold values from -6 to 6
- gate_index: int32 [6], P('grp'), parts along dimension 0, may hold values from 0 to 34
- counts: int32 [256, 256], P(('grp', 'tx')), parts along dimension 0, may hold values from 32 to 128, as said below
- voxel_column: int32 [256, 256], P(('grp', 'tx')), parts along dimension 0, may hold values from 0 to 8191, as said below
- voxel_model: float32 [64, 256, 128], P(('grp', 'tx')), parts along dimension 0, may hold values from -1 to 1
Outputs:
- adjoint_out: float32 [3, 256, 256, 128], P(None, ('grp', 'tx')), parts along dimension 1
- voxel_gradient: float32 [64, 256, 128], P(('grp', 'tx')), parts along dimension 0
There are 2 independent parts, one for each index of `grp`. A program takes and returns all parts, laid end to end along the dimension named above; each array names one. Nothing has to cross between parts.
Inputs may be any that keep to these rules, and one draw needn't show every extreme that they name: `counts`: counts reach both ends of the range in every draw. `voxel_column`: voxel column v lies on tile v // 512. Among the 2048 columns of one tx index, at most 256 map to voxel columns of any one tile, and in every draw some tile receives exactly 256 columns from every tx index. Both ends of the range are reached in every draw.
All inputs are finite; a program needn't handle non-finite values.
Results may differ from a plain program's by a relative error of at most 0.0003.
Values sent between devices are 32-bit elements; how exact they have to be, the bound alone decides.
A program may use at most 128 MiB of HBM per device.

v0:
```python
import jax
import jax.numpy as jnp
from jax import lax
from jax.sharding import PartitionSpec as P


def padded_2(value, sides, width):
    for axis, dim in sides:
        count, length = (lax.axis_size(axis), value.shape[dim])
        up = [(i, (i + 1) % count) for i in range(count - 1)]
        down = [(j, i) for i, j in up]
        last = lax.slice_in_dim(value, length - width, length, axis=dim)
        first = lax.slice_in_dim(value, 0, width, axis=dim)
        before = lax.ppermute(last, axis, up)
        after = lax.ppermute(first, axis, down)
        value = jnp.concatenate([before, value, after], axis=dim)
    return value


def passed_along(value, axis, steps):
    count = lax.axis_size(axis)
    first, last = (max(0, -steps), min(count, count - steps))
    return lax.ppermute(value, axis, [(source, source + steps) for source in range(first, last)])


def forward_diff(field, along):
    widths = [(0, 0)] * field.ndim
    widths[along] = (0, 1)
    padded = jnp.pad(field, widths)
    return lax.slice_in_dim(padded, 1, padded.shape[along], axis=along) - field


def backward_diff(field, along):
    widths = [(0, 0)] * field.ndim
    widths[along] = (1, 0)
    padded = jnp.pad(field, widths)
    return field - lax.slice_in_dim(padded, 0, field.shape[along], axis=along)


def curl_curl(field_x, field_y, field_z, inv_h, inside):
    curl_x = (forward_diff(field_z, 1) - forward_diff(field_y, 2) * inv_h) * inside
    curl_y = (forward_diff(field_x, 2) * inv_h - forward_diff(field_z, 0)) * inside
    curl_z = (forward_diff(field_y, 0) - forward_diff(field_x, 1)) * inside
    back_x = backward_diff(curl_z, 1) - backward_diff(curl_y, 2) * inv_h
    back_y = backward_diff(curl_x, 2) * inv_h - backward_diff(curl_z, 0)
    back_z = backward_diff(curl_y, 0) - backward_diff(curl_x, 1)
    return jnp.stack([back_x, back_y, back_z])


def inside_mask(first_global, length, total):
    positions = first_global + jnp.arange(length, dtype=jnp.int32)
    return ((positions >= 0) & (positions < total)).astype(jnp.float32)[:, None, None]


def regular(voxel_model):
    rimmed = padded_2(voxel_model, (("tx", 0),), 1)
    center = rimmed[1:-1]
    padded = jnp.pad(center, ((0, 0), (1, 1), (1, 1)))
    laplace = 6.0 * center - rimmed[2:] - rimmed[:-2]
    laplace = laplace - padded[:, 2:, 1:-1] - padded[:, :-2, 1:-1]
    laplace = laplace - padded[:, 1:-1, 2:] - padded[:, 1:-1, :-2]
    return 0.1 * laplace


def body(
    adjoint_in,
    forward_terms,
    log_conductivity,
    spacing,
    residuals,
    gate_index,
    counts,
    voxel_column,
    voxel_model,
):
    step_count = forward_terms.shape[0]
    cells_x = adjoint_in.shape[1]
    depth = adjoint_in.shape[3]
    tile_count = lax.axis_size("tx")
    tile_index = lax.axis_index("tx")
    total_x = cells_x * tile_count
    coefficient = 0.05 * jnp.exp(-0.7 * log_conductivity)
    inverse_sizes = 1.0 / spacing
    sources = residuals[gate_index]
    product_sum = jnp.zeros(log_conductivity.shape, jnp.float32)
    below_row = passed_along(inverse_sizes[cells_x - 1 : cells_x], "tx", 1)
    inv_rim = jnp.concatenate(
        [below_row, inverse_sizes, inverse_sizes[cells_x - 1 : cells_x]], axis=0
    )[:, :, None]
    inside = inside_mask(tile_index * cells_x - 1, cells_x + 2, total_x)
    adjoint = adjoint_in
    for step_index in range(step_count):
        extended = padded_2(adjoint, (("tx", 1),), 1)
        image = curl_curl(extended[0], extended[1], extended[2], inv_rim, inside)[:, 1:-1]
        adjoint = adjoint - coefficient[None] * image
        adjoint = adjoint.at[2, :, :, depth - 1].add(sources[step_index])
        product_sum = product_sum + jnp.sum(
            adjoint * forward_terms[step_index].astype(jnp.float32), axis=0
        )
    inside_depth = jnp.arange(depth, dtype=jnp.int32)[None, None, :] < counts[:, :, None]
    sensitivity = jnp.where(inside_depth, -0.7 * coefficient * product_sum, 0.0)
    column_count = counts.shape[0] * counts.shape[1]
    capacity = 2 * column_count // tile_count
    voxel_count = voxel_model.shape[0] * voxel_model.shape[1]
    columns = sensitivity.reshape(column_count, depth)
    voxel_ids = voxel_column.reshape(column_count)
    target = voxel_ids // voxel_count
    local_voxel = voxel_ids % voxel_count
    one_hot = (target[:, None] == jnp.arange(tile_count, dtype=jnp.int32)[None, :]).astype(
        jnp.int32
    )
    slot_rank = jnp.sum((jnp.cumsum(one_hot, axis=0) - 1) * one_hot, axis=1)
    position = target * capacity + slot_rank
    send_rows = jnp.zeros((tile_count * capacity, depth), jnp.float32).at[position].set(columns)
    send_ids = jnp.full((tile_count * capacity,), -1, jnp.int32).at[position].set(local_voxel)
    received, received_ids = (
        lax.all_to_all(
            send_rows.reshape(tile_count, capacity, depth),
            "tx",
            split_axis=0,
            concat_axis=0,
            tiled=True,
        ),
        lax.all_to_all(
            send_ids.reshape(tile_count, capacity), "tx", split_axis=0, concat_axis=0, tiled=True
        ),
    )
    received = received.reshape(tile_count * capacity, depth)
    received_ids = received_ids.reshape(tile_count * capacity)
    selector = (jnp.arange(voxel_count, dtype=jnp.int32)[:, None] == received_ids[None, :]).astype(
        jnp.float32
    )
    collected = jnp.dot(
        selector, received, precision=lax.Precision.HIGHEST, preferred_element_type=jnp.float32
    )
    collected = collected.reshape(voxel_model.shape)
    regularity = regular(voxel_model)
    return (adjoint, collected + regularity)


def solution(mesh):
    in_specs = (
        P(None, ("grp", "tx"), None, None),
        P(None, None, ("grp", "tx"), None, None),
        P(("grp", "tx"), None, None),
        P(("grp", "tx"), None),
        P(None, ("grp", "tx"), None),
        P("grp"),
        P(("grp", "tx"), None),
        P(("grp", "tx"), None),
        P(("grp", "tx"), None, None),
    )
    out_specs = (P(None, ("grp", "tx"), None, None), P(("grp", "tx"), None, None))
    return jax.shard_map(body, mesh=mesh, in_specs=in_specs, out_specs=out_specs, check_vma=False)
```

profile of v0, /device:TPU:13, one launch (start us, length us, event | category | flops | bytes accessed | tf_op | source)
XLA Modules:
  0.0 174.5 jit_solution(10438937110950553276)
XLA Ops:
  0.7 0.8 broadcast_divide_fusion
  1.5 3.7 %collective-permute-start.2 = (f32[1,256]{1,0:T(1,128)S(1)}, f32[1,256]{1,0:T(1,128)S(1)}, u32[]{:S(2)}, u32[]{:S(2)}) collective-permute-start(f32[1,256]{1,0:T(1,128)S(1)} %slice.382), channel_id=1, source_target_pairs={{0,1},{1,2},{2,3},{3,4},{4,5},{5,6},{6,7},{7,8},{8,9},{9,10},{10,1... | collective-permute-start | bytes 3080 | tf_op jit(solution)/shard_map/ppermute | solution.py:23
  5.2 1.2 fusion.116
  6.4 1.0 copy.39
  7.4 1.9 %collective-permute-start = (f32[3,1,256,128]{2,1,3,0:T(1,128)}, f32[3,1,256,128]{2,1,3,0:T(1,128)}, u32[]{:S(2)}, u32[]{:S(2)}) collective-permute-start(f32[3,1,256,128]{2,1,3,0:T(1,128)} %copy.39), channel_id=1, source_target_pairs={{0,1},{1,2},{2,3},{3,4},{4,5},{5,6},{6,7},{7,8},{8,9},{9,10},{10,1... | collective-permute-start | bytes 1179656 | tf_op jit(solution)/shard_map/ppermute | solution.py:14
  9.3 1.0 copy.40
  10.3 2.4 %collective-permute-start.1 = (f32[3,1,256,128]{2,1,3,0:T(1,128)}, f32[3,1,256,128]{2,1,3,0:T(1,128)}, u32[]{:S(2)}, u32[]{:S(2)}) collective-permute-start(f32[3,1,256,128]{2,1,3,0:T(1,128)} %copy.40), channel_id=1, source_target_pairs={{1,0},{2,1},{3,2},{4,3},{5,4},{6,5},{7,6},{8,7},{9,8},{10,9},{11,1... | collective-permute-start | bytes 1179656 | tf_op jit(solution)/shard_map/ppermute | solution.py:15
  13.2 1.4 fusion.90
  14.6 4.7 %fusion.113 = (bf16[1,3,8,256,128]{4,3,2,1,0:T(8,128)(2,1)}, bf16[1,3,8,256,128]{4,3,2,1,0:T(8,128)(2,1)}, bf16[1,3,8,256,128]{4,3,2,1,0:T(8,128)(2,1)}) fusion(bf16[3,3,8,256,128]{4,3,2,1,0:T(8,128)(2,1)} %param.16), kind=kLoop, calls=%fused_computation.198 | loop fusion | bytes 9437184 | tf_op jit(solution)/shard_map/slice | solution.py:98
  20.0 2.6 %copy.42 = f32[3,8,256,128]{2,1,3,0:T(8,128)S(1)} copy(f32[3,8,256,128]{3,2,1,0:T(8,128)} %param.15) | data formatting | bytes 6291456 | tf_op args[0]
  23.2 8.1 %reduce-window.6 = s32[16,16,128]{2,1,0:T(8,128)S(1)} reduce-window(s32[16,16,128]{2,1,0:T(8,128)} %fusion.100, s32[]{:T(128)} %constant.132.clone.1), window={size=1x1x128 pad=0_0x0_0x127_0}, to_apply=%region_0.1 | reduce-window | flops 4161536 | bytes 262148 | tf_op jit(solution)/shard_map/reduce-window
  31.4 2.4 %pad_maximum_fusion = f32[3,10,256,128]{2,1,3,0:T(8,128)S(1)} fusion(f32[3,1,256,128]{2,1,3,0:T(1,128)} %collective-permute-done.1, f32[3,8,256,128]{2,1,3,0:T(8,128)S(1)} %copy.42, f32[3,1,256,128]{2,1,3,0:T(1,128)} %collective-permute-done), kind=kLoop, calls=%fused_computation.5 | loop fusion | flops 1966080 | bytes 7864320 | tf_op jit(solution)/shard_map/concatenate | solution.py:16
  33.8 0.7 slice_bitcast_fusion.7
  34.5 1.9 %fusion.16 = (f32[10,256,128]{1,0,2:T(8,128)S(1)}, f32[10,256,128]{1,0,2:T(8,128)S(1)}, f32[10,256,128]{1,0,2:T(8,128)S(1)}) fusion(f32[10,256,128]{1,0,2:T(8,128)S(1)} %get-tuple-element.50, f32[10,256,128]{1,0,2:T(8,128)S(1)} %get-tuple-element.51, f32[10,256]{1,0:T(8,128)S(1)} %pad_maximum_fusion.11, f32[10]{0:T(128)S(1)} %and_convert_fusion, ...), kind=kLoop, calls=%fused_computation.55 | loop fusion | flops 4587520 | bytes 7874600 | tf_op jit(solution)/shard_map/mul | solution.py:42
  36.5 2.8 %fusion.20 = (f32[1,10,256,128]{2,1,3,0:T(8,128)S(1)}, f32[1,10,256,128]{2,1,3,0:T(8,128)S(1)}, f32[1,10,256,128]{2,1,3,0:T(8,128)S(1)}) fusion(f32[10,256,128]{1,0,2:T(8,128)S(1)} %get-tuple-element.72, f32[10,256,128]{1,0,2:T(8,128)S(1)} %get-tuple-element.74, f32[10,256]{1,0:T(8,128)S(1)} %pad_maximum_fusion.11, f32[10,256,128]{1,0,2:T(8,128)S(1)} %get-tuple-element.73), kind=kLoop, calls=%fused_computation.59 | loop fusion | flops 3604480 | bytes 7874560 | tf_op jit(solution)/shard_map/stack | solution.py:47
  39.3 0.7 fusion.9
  40.0 1.8 %fusion.115 = (f32[3,1,256,128]{2,1,3,0:T(1,128)}, f32[3,1,256,128]{2,1,3,0:T(1,128)}) fusion(f32[3,8,256,128]{2,1,3,0:T(8,128)S(1)} %fusion.107), kind=kLoop, calls=%fused_computation.200 | loop fusion | bytes 1572864 | tf_op jit(solution)/shard_map/slice | solution.py:12
  41.8 4.0 %collective-permute-start.3 = (f32[3,1,256,128]{2,1,3,0:T(1,128)}, f32[3,1,256,128]{2,1,3,0:T(1,128)}, u32[]{:S(2)}, u32[]{:S(2)}) collective-permute-start(f32[3,1,256,128]{2,1,3,0:T(1,128)} %get-tuple-element.62), channel_id=1, source_target_pairs={{0,1},{1,2},{2,3},{3,4},{4,5},{5,6},{6,7},{7,8},{8,9},{9,10},{10,1... | collective-permute-start | bytes 1179656 | tf_op jit(solution)/shard_map/ppermute | solution.py:14
  45.9 2.1 %collective-permute-start.4 = (f32[3,1,256,128]{2,1,3,0:T(1,128)}, f32[3,1,256,128]{2,1,3,0:T(1,128)}, u32[]{:S(2)}, u32[]{:S(2)}) collective-permute-start(f32[3,1,256,128]{2,1,3,0:T(1,128)} %get-tuple-element.63), channel_id=1, source_target_pairs={{1,0},{2,1},{3,2},{4,3},{5,4},{6,5},{7,6},{8,7},{9,8},{10,9},{11,1... | collective-permute-start | bytes 1179656 | tf_op jit(solution)/shard_map/ppermute | solution.py:15
  48.4 2.8 %copy.49 = bf16[1,3,8,256,128]{3,2,4,1,0:T(8,128)(2,1)} copy(bf16[1,3,8,256,128]{4,3,2,1,0:T(8,128)(2,1)} %get-tuple-element.54) | data formatting | bytes 3145728
  51.6 4.6 %collective-permute-done.4 = f32[3,1,256,128]{2,1,3,0:T(1,128)} collective-permute-done((f32[3,1,256,128]{2,1,3,0:T(1,128)}, f32[3,1,256,128]{2,1,3,0:T(1,128)}, u32[]{:S(2)}, u32[]{:S(2)}) %collective-permute-start.4) | collective-permute-done | bytes 393248 | tf_op jit(solution)/shard_map/ppermute | solution.py:15
  56.2 2.4 %pad_maximum_fusion.1 = f32[3,10,256,128]{2,1,3,0:T(8,128)S(1)} fusion(f32[3,1,256,128]{2,1,3,0:T(1,128)} %collective-permute-done.4, f32[3,8,256,128]{2,1,3,0:T(8,128)S(1)} %fusion.107, f32[3,1,256,128]{2,1,3,0:T(1,128)} %collective-permute-done.3), kind=kLoop, calls=%fused_computation.6 | loop fusion | flops 1966080 | bytes 7864320 | tf_op jit(solution)/shard_map/concatenate | solution.py:16
  58.6 0.7 slice_bitcast_fusion.4
  59.3 2.1 %fusion.32 = (f32[10,256,128]{1,0,2:T(8,128)S(1)}, f32[10,256,128]{1,0,2:T(8,128)S(1)}, f32[10,256,128]{1,0,2:T(8,128)S(1)}) fusion(f32[10,256,128]{1,0,2:T(8,128)S(1)} %get-tuple-element.47, f32[10,256,128]{1,0,2:T(8,128)S(1)} %get-tuple-element.48, f32[10,256]{1,0:T(8,128)S(1)} %pad_maximum_fusion.11, f32[10]{0:T(128)S(1)} %and_convert_fusion, ...), kind=kLoop, calls=%fused_computation.71 | loop fusion | flops 4587520 | bytes 7874600 | tf_op jit(solution)/shard_map/mul | solution.py:42
  61.4 2.5 %fusion.36 = (f32[1,10,256,128]{2,1,3,0:T(8,128)S(1)}, f32[1,10,256,128]{2,1,3,0:T(8,128)S(1)}, f32[1,10,256,128]{2,1,3,0:T(8,128)S(1)}) fusion(f32[10,256,128]{1,0,2:T(8,128)S(1)} %get-tuple-element.69, f32[10,256,128]{1,0,2:T(8,128)S(1)} %get-tuple-element.71, f32[10,256]{1,0:T(8,128)S(1)} %pad_maximum_fusion.11, f32[10,256,128]{1,0,2:T(8,128)S(1)} %get-tuple-element.70), kind=kLoop, calls=%fused_computation.75 | loop fusion | flops 3604480 | bytes 7874560 | tf_op jit(solution)/shard_map/stack | solution.py:47
  64.1 1.9 %fusion.12 = (f32[8,256,128]{1,0,2:T(8,128)}, f32[3,8,256,128]{2,1,3,0:T(8,128)S(1)}) fusion(f32[3,8,256,128]{2,1,3,0:T(8,128)S(1)} %copy-done.3, bf16[1,3,8,256,128]{3,2,4,1,0:T(8,128)(2,1)S(1)} %copy-done.14, f32[1,10,256,128]{2,1,3,0:T(8,128)S(1)} %get-tuple-element.80, f32[1,10,256,128]{2,1,3,0:T(8,128)S(1)} %get-tuple-element.79, ...), kind=kLoop, calls=%fused_computation.27 | loop fusion | flops 5242880 | bytes 13893632 | tf_op jit(solution)/shard_map/reduce_sum | solution.py:97
  65.9 1.4 fusion.114
  67.3 1.9 %collective-permute-start.5 = (f32[3,1,256,128]{2,1,3,0:T(1,128)}, f32[3,1,256,128]{2,1,3,0:T(1,128)}, u32[]{:S(2)}, u32[]{:S(2)}) collective-permute-start(f32[3,1,256,128]{2,1,3,0:T(1,128)} %get-tuple-element.60), channel_id=1, source_target_pairs={{0,1},{1,2},{2,3},{3,4},{4,5},{5,6},{6,7},{7,8},{8,9},{9,10},{10,1... | collective-permute-start | bytes 1179656 | tf_op jit(solution)/shard_map/ppermute | solution.py:14
  69.2 2.4 %collective-permute-start.6 = (f32[3,1,256,128]{2,1,3,0:T(1,128)}, f32[3,1,256,128]{2,1,3,0:T(1,128)}, u32[]{:S(2)}, u32[]{:S(2)}) collective-permute-start(f32[3,1,256,128]{2,1,3,0:T(1,128)} %get-tuple-element.61), channel_id=1, source_target_pairs={{1,0},{2,1},{3,2},{4,3},{5,4},{6,5},{7,6},{8,7},{9,8},{10,9},{11,1... | collective-permute-start | bytes 1179656 | tf_op jit(solution)/shard_map/ppermute | solution.py:15
  71.7 8.6 %scatter_custom_fusion = s32[4096]{0:T(1024)} fusion(s32[2048]{0:T(1024)S(1)} %bitcast.103, s32[2048]{0:T(1024)S(1)} %get-tuple-element.86, s32[]{:T(128)} %constant.131.clone.1), kind=kCustom, calls=%fused_computation.188 | custom fusion | bytes 16388 | tf_op jit(solution)/shard_map/scatter | solution.py:115
  80.3 6.5 %all-to-all-start = ((s32[16,1,256]{2,1,0:T(1,128)}), s32[16,1,256]{2,1,0:T(1,128)S(1)}, u32[]{:S(2)}, u32[]{:S(2)}) async-start(s32[16,1,256]{2,1,0:T(1,128)} %bitcast.24), calls=%async_computation | async-start | bytes 32768 | tf_op jit(solution)/shard_map/all_to_all | solution.py:124
  86.8 2.8 %copy.50 = bf16[1,3,8,256,128]{3,2,4,1,0:T(8,128)(2,1)} copy(bf16[1,3,8,256,128]{4,3,2,1,0:T(8,128)(2,1)} %get-tuple-element.53) | data formatting | bytes 3145728
  89.6 2.8 %copy.51 = bf16[1,3,8,256,128]{3,2,4,1,0:T(8,128)(2,1)} copy(bf16[1,3,8,256,128]{4,3,2,1,0:T(8,128)(2,1)} %get-tuple-element.55) | data formatting | bytes 3145728
  92.4 2.4 %pad_maximum_fusion.2 = f32[3,10,256,128]{2,1,3,0:T(8,128)S(1)} fusion(f32[3,1,256,128]{2,1,3,0:T(1,128)} %collective-permute-done.6, f32[3,8,256,128]{2,1,3,0:T(8,128)S(1)} %fusion.105, f32[3,1,256,128]{2,1,3,0:T(1,128)} %collective-permute-done.5), kind=kLoop, calls=%fused_computation.7 | loop fusion | flops 1966080 | bytes 7864320 | tf_op jit(solution)/shard_map/concatenate | solution.py:16
  94.8 0.7 slice_bitcast_fusion.1
  95.5 2.1 %fusion.48 = (f32[10,256,128]{1,0,2:T(8,128)S(1)}, f32[10,256,128]{1,0,2:T(8,128)S(1)}, f32[10,256,128]{1,0,2:T(8,128)S(1)}) fusion(f32[10,256,128]{1,0,2:T(8,128)S(1)} %get-tuple-element.44, f32[10,256,128]{1,0,2:T(8,128)S(1)} %get-tuple-element.45, f32[10,256]{1,0:T(8,128)S(1)} %pad_maximum_fusion.11, f32[10]{0:T(128)S(1)} %and_convert_fusion, ...), kind=kLoop, calls=%fused_computation.87 | loop fusion | flops 4587520 | bytes 7874600 | tf_op jit(solution)/shard_map/mul | solution.py:42
  97.6 2.8 %fusion.52 = (f32[1,10,256,128]{2,1,3,0:T(8,128)S(1)}, f32[1,10,256,128]{2,1,3,0:T(8,128)S(1)}, f32[1,10,256,128]{2,1,3,0:T(8,128)S(1)}) fusion(f32[10,256,128]{1,0,2:T(8,128)S(1)} %get-tuple-element.66, f32[10,256,128]{1,0,2:T(8,128)S(1)} %get-tuple-element.68, f32[10,256]{1,0:T(8,128)S(1)} %pad_maximum_fusion.11, f32[10,256,128]{1,0,2:T(8,128)S(1)} %get-tuple-element.67), kind=kLoop, calls=%fused_computation.91 | loop fusion | flops 3604480 | bytes 7874560 | tf_op jit(solution)/shard_map/stack | solution.py:47
  100.5 0.9 fusion.11
  102.3 1.3 copy-done.4
  103.9 0.7 copy-done.16
  105.4 7.0 %scatter_custom_fusion.1 = f32[4096,128]{1,0:T(8,128)} fusion(s32[2048]{0:T(1024)S(1)} %bitcast.104, f32[2048,128]{1,0:T(8,128)S(1)} %bitcast.94, f32[]{:T(128)} %constant.128.clone.1), kind=kCustom, calls=%fused_computation.136 | custom fusion | bytes 2097156 | tf_op jit(solution)/shard_map/scatter | solution.py:114
  112.4 6.3 %all-to-all-start.1 = ((f32[16,256,128]{2,1,0:T(8,128)}), f32[16,256,128]{2,1,0:T(8,128)}, u32[]{:S(2)}, u32[]{:S(2)}) async-start(f32[16,256,128]{2,1,0:T(8,128)} %bitcast.93), calls=%async_computation.1 | async-start | bytes 4194304 | tf_op jit(solution)/shard_map/all_to_all | solution.py:117
  118.7 0.7 fusion.117
  119.4 2.3 %collective-permute-start.7 = (f32[1,256,128]{2,1,0:T(8,128)}, f32[1,256,128]{2,1,0:T(8,128)}, u32[]{:S(2)}, u32[]{:S(2)}) collective-permute-start(f32[1,256,128]{2,1,0:T(8,128)} %get-tuple-element.84), channel_id=1, source_target_pairs={{1,0},{2,1},{3,2},{4,3},{5,4},{6,5},{7,6},{8,7},{9,8},{10,9},{11,1... | collective-permute-start | bytes 393224 | tf_op jit(solution)/shard_map/ppermute | solution.py:15
  121.7 4.5 %collective-permute-start.8 = (f32[1,256,128]{2,1,0:T(8,128)}, f32[1,256,128]{2,1,0:T(8,128)}, u32[]{:S(2)}, u32[]{:S(2)}) collective-permute-start(f32[1,256,128]{2,1,0:T(8,128)} %get-tuple-element.85), channel_id=1, source_target_pairs={{0,1},{1,2},{2,3},{3,4},{4,5},{5,6},{6,7},{7,8},{8,9},{9,10},{10,1... | collective-permute-start | bytes 393224 | tf_op jit(solution)/shard_map/ppermute | solution.py:14
  126.2 2.4 %copy.47 = f32[3,8,256,128]{3,2,1,0:T(8,128)} copy(f32[3,8,256,128]{2,1,3,0:T(8,128)S(1)} %copy-done.5) | data formatting | bytes 6291456
  128.5 39.0 %collective-permute-done.7 = f32[1,256,128]{2,1,0:T(8,128)} collective-permute-done((f32[1,256,128]{2,1,0:T(8,128)}, f32[1,256,128]{2,1,0:T(8,128)}, u32[]{:S(2)}, u32[]{:S(2)}) %collective-permute-start.7) | collective-permute-done | bytes 131104 | tf_op jit(solution)/shard_map/ppermute | solution.py:15
  167.6 6.9 %fusion.85 = f32[2,256,128]{2,1,0:T(8,128)} fusion(f32[4096,128,1]{1,0,2:T(8,128)} %bitcast.32, s32[4096]{0:T(1024)S(1)} %bitcast.102, s32[2,256]{1,0:T(2,128)S(1)} %multiply_add_fusion, f32[2,256,128]{2,1,0:T(8,128)} %param.23, f32[1,256,128]{2,1,0:T(8,128)} %collective-permute-done.8, f32[1,256,128]{2,1,0:T(8,128)} %collective-permute-done.7), kind=kOutput, calls=%fused_computation.133 | convolution fusion | flops 3224043520 | bytes 2902016 | tf_op jit(solution)/shard_map/dot_general | solution.py:133
  (76 shorter events, 4.8 us)
Async XLA Ops:
  0.6 22.0 %copy-start = (f32[35,8,256]{2,1,0:T(8,128)S(1)}, f32[35,8,256]{2,1,0:T(8,128)}, u32[]{:S(2)}) copy-start(f32[35,8,256]{2,1,0:T(8,128)} %param.19) | copy-start | bytes 860164
  0.6 12.1 %copy-start.17 = (f32[8,256,128]{2,1,0:T(8,128)S(1)}, f32[8,256,128]{2,1,0:T(8,128)}, u32[]{:S(2)}) copy-start(f32[8,256,128]{2,1,0:T(8,128)} %param.17) | copy-start | bytes 3145732
  1.5 29.9 %collective-permute-start.2 = (f32[1,256]{1,0:T(1,128)S(1)}, f32[1,256]{1,0:T(1,128)S(1)}, u32[]{:S(2)}, u32[]{:S(2)}) collective-permute-start(f32[1,256]{1,0:T(1,128)S(1)} %slice.382), channel_id=1, source_target_pairs={{0,1},{1,2},{2,3},{3,4},{4,5},{5,6},{6,7},{7,8},{8,9},{9,10},{10,1... | collective-permute-start | bytes 3080 | tf_op jit(solution)/shard_map/ppermute | solution.py:23
  7.4 24.0 %collective-permute-start = (f32[3,1,256,128]{2,1,3,0:T(1,128)}, f32[3,1,256,128]{2,1,3,0:T(1,128)}, u32[]{:S(2)}, u32[]{:S(2)}) collective-permute-start(f32[3,1,256,128]{2,1,3,0:T(1,128)} %copy.39), channel_id=1, source_target_pairs={{0,1},{1,2},{2,3},{3,4},{4,5},{5,6},{6,7},{7,8},{8,9},{9,10},{10,1... | collective-permute-start | bytes 1179656 | tf_op jit(solution)/shard_map/ppermute | solution.py:14
  10.3 21.1 %collective-permute-start.1 = (f32[3,1,256,128]{2,1,3,0:T(1,128)}, f32[3,1,256,128]{2,1,3,0:T(1,128)}, u32[]{:S(2)}, u32[]{:S(2)}) collective-permute-start(f32[3,1,256,128]{2,1,3,0:T(1,128)} %copy.40), channel_id=1, source_target_pairs={{1,0},{2,1},{3,2},{4,3},{5,4},{6,5},{7,6},{8,7},{9,8},{10,9},{11,1... | collective-permute-start | bytes 1179656 | tf_op jit(solution)/shard_map/ppermute | solution.py:15
  13.2 6.1 %copy-start.11 = (f32[8,256,128]{1,0,2:T(8,128)}, f32[8,256,128]{1,0,2:T(8,128)S(1)}, u32[]{:S(2)}) copy-start(f32[8,256,128]{1,0,2:T(8,128)S(1)} %copy.38) | copy-start | bytes 3145732
  14.6 4.7 %copy-start.19 = (s32[8,256]{1,0:T(8,128)S(1)}, s32[8,256]{1,0:T(8,128)}, u32[]{:S(2)}) copy-start(s32[8,256]{1,0:T(8,128)} %param.22) | copy-start | bytes 24580
  14.6 5.4 %copy-start.21 = (s32[3]{0:T(128)S(1)}, s32[3]{0:T(128)}, u32[]{:S(2)}) copy-start(s32[3]{0:T(128)} %param.20) | copy-start | bytes 40
  22.7 11.1 %copy-start.6 = (f32[3,8,256,128]{2,1,3,0:T(8,128)}, f32[3,8,256,128]{2,1,3,0:T(8,128)S(1)}, u32[]{:S(2)}) copy-start(f32[3,8,256,128]{2,1,3,0:T(8,128)S(1)} %copy.42) | copy-start | bytes 9437188
  36.4 2.9 %copy-start.7 = (f32[3,8,256,128]{2,1,3,0:T(8,128)S(1)}, f32[3,8,256,128]{2,1,3,0:T(8,128)}, u32[]{:S(2)}) copy-start(f32[3,8,256,128]{2,1,3,0:T(8,128)} %copy-done.6) | copy-start | bytes 9437188
  36.5 2.9 %copy-start.8 = (f32[8,256,128]{1,0,2:T(8,128)S(1)}, f32[8,256,128]{1,0,2:T(8,128)}, u32[]{:S(2)}) copy-start(f32[8,256,128]{1,0,2:T(8,128)} %fusion.90) | copy-start | bytes 3145732
  40.0 16.2 %copy-start.2 = (f32[3,8,256,128]{2,1,3,0:T(8,128)}, f32[3,8,256,128]{2,1,3,0:T(8,128)S(1)}, u32[]{:S(2)}) copy-start(f32[3,8,256,128]{2,1,3,0:T(8,128)S(1)} %fusion.107) | copy-start | bytes 9437188
  41.8 9.8 %collective-permute-start.3 = (f32[3,1,256,128]{2,1,3,0:T(1,128)}, f32[3,1,256,128]{2,1,3,0:T(1,128)}, u32[]{:S(2)}, u32[]{:S(2)}) collective-permute-start(f32[3,1,256,128]{2,1,3,0:T(1,128)} %get-tuple-element.62), channel_id=1, source_target_pairs={{0,1},{1,2},{2,3},{3,4},{4,5},{5,6},{6,7},{7,8},{8,9},{9,10},{10,1... | collective-permute-start | bytes 1179656 | tf_op jit(solution)/shard_map/ppermute | solution.py:14
  45.9 10.3 %collective-permute-start.4 = (f32[3,1,256,128]{2,1,3,0:T(1,128)}, f32[3,1,256,128]{2,1,3,0:T(1,128)}, u32[]{:S(2)}, u32[]{:S(2)}) collective-permute-start(f32[3,1,256,128]{2,1,3,0:T(1,128)} %get-tuple-element.63), channel_id=1, source_target_pairs={{1,0},{2,1},{3,2},{4,3},{5,4},{6,5},{7,6},{8,7},{9,8},{10,9},{11,1... | collective-permute-start | bytes 1179656 | tf_op jit(solution)/shard_map/ppermute | solution.py:15
  61.4 2.6 %copy-start.3 = (f32[3,8,256,128]{2,1,3,0:T(8,128)S(1)}, f32[3,8,256,128]{2,1,3,0:T(8,128)}, u32[]{:S(2)}) copy-start(f32[3,8,256,128]{2,1,3,0:T(8,128)} %copy-done.2) | copy-start | bytes 9437188
  61.4 2.6 %copy-start.9 = (f32[8,256,128]{1,0,2:T(8,128)S(1)}, f32[8,256,128]{1,0,2:T(8,128)}, u32[]{:S(2)}) copy-start(f32[8,256,128]{1,0,2:T(8,128)} %fusion.90) | copy-start | bytes 3145732
  61.4 2.7 %copy-start.14 = (bf16[1,3,8,256,128]{3,2,4,1,0:T(8,128)(2,1)S(1)}, bf16[1,3,8,256,128]{3,2,4,1,0:T(8,128)(2,1)}, u32[]{:S(2)}) copy-start(bf16[1,3,8,256,128]{3,2,4,1,0:T(8,128)(2,1)} %copy.49) | copy-start | bytes 4718596
  67.3 25.1 %collective-permute-start.5 = (f32[3,1,256,128]{2,1,3,0:T(1,128)}, f32[3,1,256,128]{2,1,3,0:T(1,128)}, u32[]{:S(2)}, u32[]{:S(2)}) collective-permute-start(f32[3,1,256,128]{2,1,3,0:T(1,128)} %get-tuple-element.60), channel_id=1, source_target_pairs={{0,1},{1,2},{2,3},{3,4},{4,5},{5,6},{6,7},{7,8},{8,9},{9,10},{10,1... | collective-permute-start | bytes 1179656 | tf_op jit(solution)/shard_map/ppermute | solution.py:14
  69.2 23.1 %collective-permute-start.6 = (f32[3,1,256,128]{2,1,3,0:T(1,128)}, f32[3,1,256,128]{2,1,3,0:T(1,128)}, u32[]{:S(2)}, u32[]{:S(2)}) collective-permute-start(f32[3,1,256,128]{2,1,3,0:T(1,128)} %get-tuple-element.61), channel_id=1, source_target_pairs={{1,0},{2,1},{3,2},{4,3},{5,4},{6,5},{7,6},{8,7},{9,8},{10,9},{11,1... | collective-permute-start | bytes 1179656 | tf_op jit(solution)/shard_map/ppermute | solution.py:15
  80.3 32.1 %all-to-all-start = ((s32[16,1,256]{2,1,0:T(1,128)}), s32[16,1,256]{2,1,0:T(1,128)S(1)}, u32[]{:S(2)}, u32[]{:S(2)}) async-start(s32[16,1,256]{2,1,0:T(1,128)} %bitcast.24), calls=%async_computation | async-start | bytes 32768 | tf_op jit(solution)/shard_map/all_to_all | solution.py:124
  97.6 2.8 %copy-start.10 = (f32[8,256,128]{1,0,2:T(8,128)S(1)}, f32[8,256,128]{1,0,2:T(8,128)}, u32[]{:S(2)}) copy-start(f32[8,256,128]{1,0,2:T(8,128)} %fusion.90) | copy-start | bytes 3145732
  97.6 2.8 %copy-start.15 = (bf16[1,3,8,256,128]{3,2,4,1,0:T(8,128)(2,1)S(1)}, bf16[1,3,8,256,128]{3,2,4,1,0:T(8,128)(2,1)}, u32[]{:S(2)}) copy-start(bf16[1,3,8,256,128]{3,2,4,1,0:T(8,128)(2,1)} %copy.50) | copy-start | bytes 4718596
  100.5 1.4 copy-start.13
  101.9 1.7 copy-start.4
  101.9 2.0 %copy-start.12 = (f32[8,256,128]{1,0,2:T(8,128)S(1)}, f32[8,256,128]{1,0,2:T(8,128)}, u32[]{:S(2)}) copy-start(f32[8,256,128]{1,0,2:T(8,128)} %copy-done.11) | copy-start | bytes 3145732
  101.9 2.7 %copy-start.16 = (f32[8,256,128]{1,0,2:T(8,128)S(1)}, f32[8,256,128]{1,0,2:T(8,128)}, u32[]{:S(2)}) copy-start(f32[8,256,128]{1,0,2:T(8,128)} %get-tuple-element.58) | copy-start | bytes 3145732
  101.9 2.7 %copy-start.20 = (s32[8,256]{1,0:T(8,128)S(1)}, s32[8,256]{1,0:T(8,128)}, u32[]{:S(2)}) copy-start(s32[8,256]{1,0:T(8,128)} %param.21) | copy-start | bytes 24580
  112.4 6.3 %copy-start.18 = (f32[2,256,128]{2,1,0:T(8,128)S(1)}, f32[2,256,128]{2,1,0:T(8,128)}, u32[]{:S(2)}) copy-start(f32[2,256,128]{2,1,0:T(8,128)} %param.23) | copy-start | bytes 786436
  112.4 13.7 %copy-start.5 = (f32[3,8,256,128]{2,1,3,0:T(8,128)S(1)}, f32[3,8,256,128]{2,1,3,0:T(8,128)}, u32[]{:S(2)}) copy-start(f32[3,8,256,128]{2,1,3,0:T(8,128)} %copy-done.4) | copy-start | bytes 9437188
  112.4 55.2 %all-to-all-start.1 = ((f32[16,256,128]{2,1,0:T(8,128)}), f32[16,256,128]{2,1,0:T(8,128)}, u32[]{:S(2)}, u32[]{:S(2)}) async-start(f32[16,256,128]{2,1,0:T(8,128)} %bitcast.93), calls=%async_computation.1 | async-start | bytes 4194304 | tf_op jit(solution)/shard_map/all_to_all | solution.py:117
  119.4 48.2 %collective-permute-start.7 = (f32[1,256,128]{2,1,0:T(8,128)}, f32[1,256,128]{2,1,0:T(8,128)}, u32[]{:S(2)}, u32[]{:S(2)}) collective-permute-start(f32[1,256,128]{2,1,0:T(8,128)} %get-tuple-element.84), channel_id=1, source_target_pairs={{1,0},{2,1},{3,2},{4,3},{5,4},{6,5},{7,6},{8,7},{9,8},{10,9},{11,1... | collective-permute-start | bytes 393224 | tf_op jit(solution)/shard_map/ppermute | solution.py:15
  121.7 45.9 %collective-permute-start.8 = (f32[1,256,128]{2,1,0:T(8,128)}, f32[1,256,128]{2,1,0:T(8,128)}, u32[]{:S(2)}, u32[]{:S(2)}) collective-permute-start(f32[1,256,128]{2,1,0:T(8,128)} %get-tuple-element.85), channel_id=1, source_target_pairs={{0,1},{1,2},{2,3},{3,4},{4,5},{5,6},{6,7},{7,8},{8,9},{9,10},{10,1... | collective-permute-start | bytes 393224 | tf_op jit(solution)/shard_map/ppermute | solution.py:14
  167.6 6.9 %copy-start.1 = (f32[35,8,256]{2,1,0:T(8,128)S(1)}, f32[35,8,256]{2,1,0:T(8,128)}, u32[]{:S(2)}) copy-start(f32[35,8,256]{2,1,0:T(8,128)} %param.19) | copy-start | bytes 860164
where the time goes:
time: 176 us; the launch traced here: 175 us
  local copies, waits for them, and re-layouts  47.6 us (27%)
  waiting for transfers between devices  43.6 us (25%)
  starting transfers between devices  37.9 us (22%)
  other arithmetic  37.2 us (21%)
  matrix products  6.93 us (4%)
    ppermute x4, waiting for transfers between devices, padded_2(): after = lax.ppermute(first, axis, down)  43.6 us
    unnamed x52, local copies, waits for them, and re-layouts  16.8 us
    ppermute x4, starting transfers between devices, padded_2(): before = lax.ppermute(last, axis, up)  12.3 us
    ppermute x4, starting transfers between devices, padded_2(): after = lax.ppermute(first, axis, down)  9.16 us
    scatter x1, local copies, waits for them, and re-layouts, body(): jnp.full((tile_count * capacity,), -1, jnp.int32).at[position]  8.62 us
    another operation x2, other arithmetic  8.3 us
    another operation x3, other arithmetic, curl_curl(): return jnp.stack([back_x, back_y, back_z])  8.17 us
    concatenate x3, other arithmetic, padded_2(): value = jnp.concatenate([before, value, after], axis=dim)  7.11 us
  transfers between devices with their start and end apart: 11, of which 2 were waited for; matrix products, arithmetic and copies ran while one was open for 34% of the time, Pallas kernels for 0%

commit v1 on v0

v1 whole, which is shorter than its diff:
```python
import functools

import jax
import jax.numpy as jnp
from jax import lax
from jax.experimental import pallas as pl
from jax.experimental.pallas import tpu as pltpu
from jax.sharding import PartitionSpec as P

MESH = pl.DeviceIdType.MESH


def lane_index(shape):
    return lax.broadcasted_iota(jnp.int32, shape, 1)


def next_z(value):
    depth = value.shape[1]
    return jnp.where(lane_index(value.shape) < depth - 1, pltpu.roll(value, depth - 1, 1), 0.0)


def last_z(value):
    return jnp.where(lane_index(value.shape) > 0, pltpu.roll(value, 1, 1), 0.0)


def field_kernel(
    n,
    adj_ref,
    fwd_ref,
    logc_ref,
    spacing_ref,
    residual_ref,
    gate_ref,
    counts_ref,
    model_ref,
    out_ref,
    sens_ref,
    reg_ref,
    field,
    curl,
    coef,
    inv,
    total,
    terms,
    columns,
    from_low,
    from_high,
    to_high,
    model,
    model_low,
    model_high,
    local_sem,
    term_sem,
    send_up,
    send_down,
    recv_low,
    recv_high,
    model_send,
    model_recv,
):
    steps = fwd_ref.shape[0]
    cells, ny, nz = logc_ref.shape
    rows_v = model_ref.shape[0]
    grp, me = lax.axis_index("grp"), lax.axis_index("tx")
    low, high = lax.rem(me + n - 1, n), lax.rem(me + 1, n)
    has_low, has_high = me > 0, me < n - 1
    chunk = 64
    chunks = [(y, chunk) for y in range(0, ny, chunk)]

    load_last = pltpu.make_async_copy(
        adj_ref.at[:, pl.ds(cells - 1, 1)], field.at[:, pl.ds(cells - 1, 1), pl.ds(0, ny)], local_sem.at[0]
    )
    load_last.start()
    load_rest = pltpu.make_async_copy(
        adj_ref.at[:, pl.ds(0, cells - 1)], field.at[:, pl.ds(0, cells - 1), pl.ds(0, ny)], local_sem.at[1]
    )
    load_rest.start()
    load_coef = pltpu.make_async_copy(logc_ref, coef, local_sem.at[2])
    load_coef.start()
    load_terms = [pltpu.make_async_copy(fwd_ref.at[s], terms.at[s], term_sem.at[s]) for s in range(steps)]
    for copy in load_terms:
        copy.start()

    barrier = pltpu.get_barrier_semaphore()
    for neighbour in (low, high):
        pl.semaphore_signal(barrier, inc=1, device_id=(grp, neighbour), device_id_type=MESH)

    inverse = 1.0 / spacing_ref[...]
    depth_count = counts_ref[...].astype(jnp.float32)
    sources = [residual_ref[gate_ref[s]] for s in range(steps)]
    for y in range(0, ny, nz):
        parts = [v[:, y : y + nz] for v in [inverse, depth_count] + sources]
        parts.append(jnp.zeros((nz - cells * (2 + steps), nz), jnp.float32))
        columns[pl.ds(y, nz), :] = jnp.concatenate(parts, axis=0).T

    for x in range(cells):
        inv[x] = jnp.broadcast_to(columns[:, x : x + 1], (ny, nz))
        for a in range(3):
            field[a, x, pl.ds(ny, 8), :] = jnp.zeros((8, nz), jnp.float32)
            curl[a, x + 1, pl.ds(0, 8), :] = jnp.zeros((8, nz), jnp.float32)

    def copy_up(slot):
        return pltpu.make_async_remote_copy(
            src_ref=to_high.at[slot],
            dst_ref=from_low.at[slot],
            send_sem=send_up.at[slot],
            recv_sem=recv_low.at[slot],
            device_id=(grp, high),
            device_id_type=MESH,
        )

    def copy_down(slot):
        return pltpu.make_async_remote_copy(
            src_ref=field.at[pl.ds(1, 2), 0, pl.ds(0, ny)],
            dst_ref=from_high.at[slot],
            send_sem=send_down.at[slot],
            recv_sem=recv_high.at[slot],
            device_id=(grp, low),
            device_id_type=MESH,
        )

    def send_high(slot):
        x = cells - 1
        for y, size in chunks:
            e0, e1, e2 = (field[a, x, pl.ds(y, size), :] for a in range(3))
            e0y = field[0, x, pl.ds(y + 1, size), :]
            to_high[slot, 0, pl.ds(y, size), :] = inv[x, pl.ds(y, size), :] * (next_z(e0) - e0) + e2
            to_high[slot, 1, pl.ds(y, size), :] = (e0 - e0y) - e1

        @pl.when(has_high)
        def _():
            copy_up(slot).start()

    def send_low(slot):
        @pl.when(has_low)
        def _():
            copy_down(slot).start()

    def curl_row(x, next_row):
        for y, size in chunks:
            at = pl.ds(y, size)
            e0, e1, e2 = (field[a, x, at, :] for a in range(3))
            e0y, e2y = field[0, x, pl.ds(y + 1, size), :], field[2, x, pl.ds(y + 1, size), :]
            e1x, e2x = next_row(at)
            h = inv[x, at, :]
            to = pl.ds(y + 8, size)
            curl[0, x + 1, to, :] = (e2y - e2) - h * (next_z(e1) - e1)
            curl[1, x + 1, to, :] = h * (next_z(e0) - e0) - (e2x - e2)
            curl[2, x + 1, to, :] = (e1x - e1) - (e0y - e0)

    def update_row(s, x):
        for y, size in chunks:
            at, to, before = pl.ds(y, size), pl.ds(y + 8, size), pl.ds(y + 7, size)
            h, c = inv[x, at, :], coef[x, at, :]
            h0, h1, h2 = (curl[a, x + 1, to, :] for a in range(3))
            h0y, h2y = curl[0, x + 1, before, :], curl[2, x + 1, before, :]
            h1x, h2x = curl[1, x, to, :], curl[2, x, to, :]
            image = (
                (h2 - h2y) - h * (h1 - last_z(h1)),
                h * (h0 - last_z(h0)) - (h2 - h2x),
                (h1 - h1x) - (h0 - h0y),
            )
            shift = nz - 1 - (2 + s) * cells - x
            source = pltpu.roll(columns[at, :], shift, 1)
            source = jnp.where(lane_index(source.shape) == nz - 1, source, 0.0)
            for a in range(3):
                value = field[a, x, at, :] - c * image[a]
                field[a, x, at, :] = value + source if a == 2 else value

    def product_row(s, x):
        for y, size in chunks:
            at = pl.ds(y, size)
            value = sum(field[a, x, at, :] * terms[s, a, x, at, :].astype(jnp.float32) for a in range(3))
            total[x, at, :] = value if s == 0 else total[x, at, :] + value

    pl.semaphore_wait(barrier, 2)
    load_last.wait()
    send_high(0)
    load_rest.wait()
    send_low(0)

    def model_up():
        return pltpu.make_async_remote_copy(
            src_ref=model_ref.at[rows_v - 1],
            dst_ref=model_low,
            send_sem=model_send.at[0],
            recv_sem=model_recv.at[0],
            device_id=(grp, high),
            device_id_type=MESH,
        )

    def model_down():
        return pltpu.make_async_remote_copy(
            src_ref=model_ref.at[0],
            dst_ref=model_high,
            send_sem=model_send.at[1],
            recv_sem=model_recv.at[1],
            device_id=(grp, low),
            device_id_type=MESH,
        )

    @pl.when(has_high)
    def _():
        model_up().start()

    @pl.when(has_low)
    def _():
        model_down().start()

    load_coef.wait()

    def coefficient_row(x, carry):
        coef[x] = 0.05 * jnp.exp(-0.7 * coef[x])
        return carry

    lax.fori_loop(0, cells, coefficient_row, 0)

    @pl.when(jnp.logical_not(has_low))
    def _():
        model_low[...] = jnp.zeros_like(model_low)

    @pl.when(jnp.logical_not(has_high))
    def _():
        model_high[...] = jnp.zeros_like(model_high)
        for s in range(steps):
            from_high[s] = jnp.zeros(from_high.shape[1:], jnp.float32)

    def regularize():
        @pl.when(has_high)
        def _():
            model_up().wait_send()
            model_down().wait_recv()

        @pl.when(has_low)
        def _():
            model_down().wait_send()
            model_up().wait_recv()

        for v in range(rows_v):
            model[v, pl.ds(0, 8), :] = jnp.zeros((8, nz), jnp.float32)
            model[v, pl.ds(ny + 8, 8), :] = jnp.zeros((8, nz), jnp.float32)
            model[v, pl.ds(8, ny), :] = model_ref[v]
        for v in range(rows_v):
            for y, size in chunks:
                at = pl.ds(y, size)
                center = model_ref[v, at, :]
                below = model_low[at, :] if v == 0 else model_ref[v - 1, at, :]
                above = model_high[at, :] if v == rows_v - 1 else model_ref[v + 1, at, :]
                sides = model[v, pl.ds(y + 7, size), :] + model[v, pl.ds(y + 9, size), :]
                around = below + above + sides + next_z(center) + last_z(center)
                reg_ref[v, at, :] = 0.1 * (6.0 * center - around)

    def store(first, count, sem):
        return pltpu.make_async_copy(
            field.at[:, pl.ds(first, count), pl.ds(0, ny)], out_ref.at[:, pl.ds(first, count)], local_sem.at[sem]
        )

    for s in range(steps):

        def inner_curl(x, carry):
            curl_row(x, lambda at: (field[1, x + 1, at, :], field[2, x + 1, at, :]))
            return carry

        lax.fori_loop(0, cells - 1, inner_curl, 0)
        if s > 0:

            def late_product(x, carry):
                product_row(s - 1, x)
                return carry

            load_terms[s - 1].wait()
            lax.fori_loop(0, cells, late_product, 0)

        def inner_update(x, carry):
            update_row(s, x)
            return carry

        lax.fori_loop(1, cells - 1, inner_update, 0)
        if s == steps - 1:
            store(1, cells - 2, 3).start()
        if s == min(1, steps - 1):
            regularize()

        @pl.when(has_high)
        def _():
            copy_up(s).wait_send()
            copy_down(s).wait_recv()

        @pl.when(has_low)
        def _():
            copy_down(s).wait_send()
            copy_up(s).wait_recv()

        curl_row(cells - 1, lambda at: (from_high[s, 0, at, :], from_high[s, 1, at, :]))

        @pl.when(has_low)
        def _():
            for y, size in chunks:
                at, to = pl.ds(y, size), pl.ds(y + 8, size)
                curl[1, 0, to, :] = from_low[s, 0, at, :] - field[2, 0, at, :]
                curl[2, 0, to, :] = from_low[s, 1, at, :] + field[1, 0, at, :]

        @pl.when(jnp.logical_not(has_low))
        def _():
            for a in (1, 2):
                curl[a, 0] = jnp.zeros(curl.shape[2:], jnp.float32)

        update_row(s, cells - 1)
        if s < steps - 1:
            send_high(s + 1)
        update_row(s, 0)
        if s < steps - 1:
            send_low(s + 1)
    store(0, 1, 4).start()
    store(cells - 1, 1, 5).start()

    load_terms[steps - 1].wait()
    for x in range(cells):
        product_row(steps - 1, x)
        inside = lane_index((ny, nz)).astype(jnp.float32) < jnp.broadcast_to(
            columns[:, cells + x : cells + x + 1], (ny, nz)
        )
        sens_ref[x] = jnp.where(inside, -0.7 * coef[x] * total[x], 0.0)
    store(1, cells - 2, 3).wait()
    store(0, 1, 4).wait()
    store(cells - 1, 1, 5).wait()


def field_phase(n, adj, fwd, logc, spacing, residuals, gates, counts, model):
    steps = fwd.shape[0]
    cells, ny, nz = logc.shape
    f32 = jnp.float32
    anywhere, vmem = pl.BlockSpec(memory_space=pl.ANY), pl.BlockSpec(memory_space=pltpu.VMEM)
    dma = pltpu.SemaphoreType.DMA
    return pl.pallas_call(
        functools.partial(field_kernel, n),
        out_shape=(
            jax.ShapeDtypeStruct(adj.shape, f32),
            jax.ShapeDtypeStruct(logc.shape, f32),
            jax.ShapeDtypeStruct(model.shape, f32),
        ),
        in_specs=[anywhere] * 3 + [vmem, vmem, pl.BlockSpec(memory_space=pltpu.SMEM), vmem, vmem],
        out_specs=(anywhere, vmem, vmem),
        scratch_shapes=[
            pltpu.VMEM((3, cells, ny + 8, nz), f32),
            pltpu.VMEM((3, cells + 1, ny + 8, nz), f32),
            pltpu.VMEM((cells, ny, nz), f32),
            pltpu.VMEM((cells, ny, nz), f32),
            pltpu.VMEM((cells, ny, nz), f32),
            pltpu.VMEM(fwd.shape, jnp.bfloat16),
            pltpu.VMEM((ny, nz), f32),
            pltpu.VMEM((steps, 2, ny, nz), f32),
            pltpu.VMEM((steps, 2, ny, nz), f32),
            pltpu.VMEM((steps, 2, ny, nz), f32),
            pltpu.VMEM((model.shape[0], ny + 16, nz), f32),
            pltpu.VMEM((ny, nz), f32),
            pltpu.VMEM((ny, nz), f32),
            dma((6,)),
            dma((steps,)),
            dma((steps,)),
            dma((steps,)),
            dma((steps,)),
            dma((steps,)),
            dma((2,)),
            dma((2,)),
        ],
        compiler_params=pltpu.CompilerParams(collective_id=0, has_side_effects=True, vmem_limit_bytes=48 << 20),
    )(adj, fwd, logc, spacing, residuals, gates, counts, model)


def body(
    adjoint_in,
    forward_terms,
    log_conductivity,
    spacing,
    residuals,
    gate_index,
    counts,
    voxel_column,
    voxel_model,
):
    depth = adjoint_in.shape[3]
    tile_count = lax.axis_size("tx")
    adjoint, sensitivity, regularity = field_phase(
        tile_count,
        adjoint_in,
        forward_terms,
        log_conductivity,
        spacing,
        residuals,
        gate_index,
        counts,
        voxel_model,
    )
    column_count = counts.shape[0] * counts.shape[1]
    capacity = 2 * column_count // tile_count
    voxel_count = voxel_model.shape[0] * voxel_model.shape[1]
    columns = sensitivity.reshape(column_count, depth)
    voxel_ids = voxel_column.reshape(column_count)
    target = voxel_ids // voxel_count
    local_voxel = voxel_ids % voxel_count
    one_hot = (target[:, None] == jnp.arange(tile_count, dtype=jnp.int32)[None, :]).astype(
        jnp.int32
    )
    slot_rank = jnp.sum((jnp.cumsum(one_hot, axis=0) - 1) * one_hot, axis=1)
    position = target * capacity + slot_rank
    send_rows = jnp.zeros((tile_count * capacity, depth), jnp.float32).at[position].set(columns)
    send_ids = jnp.full((tile_count * capacity,), -1, jnp.int32).at[position].set(local_voxel)
    received, received_ids = (
        lax.all_to_all(
            send_rows.reshape(tile_count, capacity, depth),
            "tx",
            split_axis=0,
            concat_axis=0,
            tiled=True,
        ),
        lax.all_to_all(
            send_ids.reshape(tile_count, capacity), "tx", split_axis=0, concat_axis=0, tiled=True
        ),
    )
    received = received.reshape(tile_count * capacity, depth)
    received_ids = received_ids.reshape(tile_count * capacity)
    selector = (jnp.arange(voxel_count, dtype=jnp.int32)[:, None] == received_ids[None, :]).astype(
        jnp.float32
    )
    collected = jnp.dot(
        selector, received, precision=lax.Precision.HIGHEST, preferred_element_type=jnp.float32
    )
    collected = collected.reshape(voxel_model.shape)
    return (adjoint, collected + regularity)


def solution(mesh):
    in_specs = (
        P(None, ("grp", "tx"), None, None),
        P(None, None, ("grp", "tx"), None, None),
        P(("grp", "tx"), None, None),
        P(("grp", "tx"), None),
        P(None, ("grp", "tx"), None),
        P("grp"),
        P(("grp", "tx"), None),
        P(("grp", "tx"), None),
        P(("grp", "tx"), None, None),
    )
    out_specs = (P(None, ("grp", "tx"), None, None), P(("grp", "tx"), None, None))
    return jax.shard_map(body, mesh=mesh, in_specs=in_specs, out_specs=out_specs, check_vma=False)
```

time: 176 us -> 126 us (0.72)
  the two profiles are of different devices: /device:TPU:13 before, /device:TPU:15 now
where the time goes in v1:
time: 126 us
  waiting for transfers between devices  47.5 us (38%)
  local copies, waits for them, and re-layouts  26.3 us (21%)
  Pallas kernels  23.2 us (18%)
  starting transfers between devices  16.8 us (13%)
  matrix products  6.18 us (5%)
  other arithmetic  4.98 us (4%)
    all_to_all x1, waiting for transfers between devices, body(): lax.all_to_all(send_rows.reshape(tile_count, capacity, depth), 'tx', spli...  47.5 us
    pallas_call x1, Pallas kernels, field_phase(): pl.pallas_call(functools.partial(field_kernel, n), out_shape=(jax.ShapeDt...  23.2 us
    all_to_all x1, starting transfers between devices, body(): lax.all_to_all(send_rows.reshape(tile_count, capacity, depth), 'tx', spli...  10.3 us
    unnamed x17, local copies, waits for them, and re-layouts  9.23 us
    scatter x1, local copies, waits for them, and re-layouts, body(): jnp.full((tile_count * capacity,), -1, jnp.int32).at[position]  8.62 us
    scatter x1, local copies, waits for them, and re-layouts, body(): jnp.zeros((tile_count * capacity, depth), jnp.float32).at[position]  7.36 us
    all_to_all x1, starting transfers between devices, body(): lax.all_to_all(send_ids.reshape(tile_count, capacity), 'tx', split_axis=0...  6.55 us
    dot_general x1, matrix products, body(): jnp.dot(selector, received, precision=lax.Precision.HIGHEST, preferred_el...  6.18 us
  transfers between devices with their start and end apart: 2, of which 1 were waited for; matrix products, arithmetic and copies ran while one was open for 6% of the time, Pallas kernels for 18%

profile of v1, /device:TPU:15, one launch (start us, length us, event | category | flops | bytes accessed | tf_op | source)
XLA Modules:
  0.0 125.7 jit_solution(12494109840724948389)
XLA Ops:
  0.6 0.7 reshape.167
  1.4 4.5 %reduce-window.6 = s32[16,16,128]{2,1,0:T(8,128)S(1)} reduce-window(s32[16,16,128]{2,1,0:T(8,128)S(1)} %fusion.11, s32[]{:T(128)} %constant.38.clone.1), window={size=1x1x128 pad=0_0x0_0x127_0}, to_apply=%region_0.1 | reduce-window | flops 4161536 | bytes 262148 | tf_op jit(solution)/shard_map/reduce-window
  5.9 0.4 slice_reduce_fusion
  6.3 0.2 reduce-window.9
  6.5 0.1 add_add_fusion
  6.6 0.7 copy.12
  7.3 0.7 copy.11
  8.1 0.1 fusion.10
  8.1 0.1 compare_select_fusion
  8.2 8.6 %scatter_custom_fusion = s32[4096]{0:T(1024)} fusion(s32[2048]{0:T(1024)S(1)} %bitcast.40, s32[2048]{0:T(1024)S(1)} %get-tuple-element.8, s32[]{:T(128)} %constant.36.clone.1), kind=kCustom, calls=%fused_computation.34 | custom fusion | bytes 16388 | tf_op jit(solution)/shard_map/scatter | solution.py:408
  16.8 6.6 %all-to-all-start = ((s32[16,1,256]{2,1,0:T(1,128)}), s32[16,1,256]{2,1,0:T(1,128)S(1)}, u32[]{:S(2)}, u32[]{:S(2)}) async-start(s32[16,1,256]{2,1,0:T(1,128)} %bitcast.3), calls=%async_computation | async-start | bytes 32768 | tf_op jit(solution)/shard_map/all_to_all | solution.py:417
  23.4 0.0 copy-start
  23.4 1.2 copy-done
  24.6 0.0 copy-start.1
  24.6 1.0 copy-done.1
  25.5 0.0 copy-start.2
  25.6 0.9 copy-done.2
  26.5 0.0 copy-start.3
  26.5 0.7 copy-done.3
  27.2 0.0 copy-start.4
  27.2 0.7 copy-done.4
  27.9 0.0 copy-start.5
  27.9 0.7 copy-done.5
  28.5 23.2 %shard_map.104 = (f32[3,8,256,128]{3,2,1,0:T(8,128)S(1)}, f32[8,256,128]{2,1,0:T(8,128)S(1)}, f32[2,256,128]{2,1,0:T(8,128)S(1)}) custom-call(f32[3,8,256,128]{3,2,1,0:T(8,128)} %adj_ref.1, bf16[3,3,8,256,128]{4,3,2,1,0:T(8,128)(2,1)} %fwd_ref.1, f32[8,256,128]{2,1,0:T(8,128)S(1)} %copy-done, f32[8,256]{1,0:T(8,128)S(1)} %copy-done.3, ...), custom_call_target="tpu_custom_call" | custom-call | tf_op jit(solution)/shard_map/pallas_call | solution.py:335
  51.7 0.0 copy-start.6
  51.7 1.0 copy-done.6
  52.7 7.4 %scatter_custom_fusion.1 = f32[4096,128]{1,0:T(8,128)} fusion(s32[2048]{0:T(1024)S(1)} %bitcast.41, f32[2048,128]{1,0:T(8,128)} %bitcast.30, f32[]{:T(128)} %constant.43.clone.1), kind=kCustom, calls=%fused_computation.7 | custom fusion | bytes 2097664 | tf_op jit(solution)/shard_map/scatter | solution.py:407
  60.1 0.0 all-to-all-done
  60.1 10.3 %all-to-all-start.1 = ((f32[16,256,128]{2,1,0:T(8,128)}), f32[16,256,128]{2,1,0:T(8,128)}, u32[]{:S(2)}, u32[]{:S(2)}) async-start(f32[16,256,128]{2,1,0:T(8,128)} %bitcast.31), calls=%async_computation.1 | async-start | bytes 4194304 | tf_op jit(solution)/shard_map/all_to_all | solution.py:410
  70.3 47.5 %all-to-all-done.1 = f32[16,256,128]{2,1,0:T(8,128)} async-done(((f32[16,256,128]{2,1,0:T(8,128)}), f32[16,256,128]{2,1,0:T(8,128)}, u32[]{:S(2)}, u32[]{:S(2)}) %all-to-all-start.1) | async-done | bytes 2097184 | tf_op jit(solution)/shard_map/all_to_all | solution.py:410
  117.9 6.2 %fusion.4 = f32[2,256,128]{2,1,0:T(8,128)} fusion(f32[2,256,128]{2,1,0:T(8,128)S(1)} %get-tuple-element.7, f32[4096,128,1]{1,0,2:T(8,128)} %bitcast.8, s32[4096]{0:T(1024)S(1)} %bitcast.39, s32[2,256]{1,0:T(2,128)S(1)} %multiply_add_fusion), kind=kOutput, calls=%fused_computation.6 | convolution fusion | flops 3223388160 | bytes 2639872 | tf_op jit(solution)/shard_map/dot_general | solution.py:426
  124.0 1.7 %copy.16 = f32[3,8,256,128]{3,2,1,0:T(8,128)} copy(f32[3,8,256,128]{3,2,1,0:T(8,128)S(1)} %get-tuple-element.12) | data formatting | bytes 6291456
  (4 shorter events, 0.0 us)
Async XLA Ops:
  16.8 43.3 %all-to-all-start = ((s32[16,1,256]{2,1,0:T(1,128)}), s32[16,1,256]{2,1,0:T(1,128)S(1)}, u32[]{:S(2)}, u32[]{:S(2)}) async-start(s32[16,1,256]{2,1,0:T(1,128)} %bitcast.3), calls=%async_computation | async-start | bytes 32768 | tf_op jit(solution)/shard_map/all_to_all | solution.py:417
  23.4 1.2 copy-start
  24.6 1.0 copy-start.1
  25.5 0.9 copy-start.2
  26.5 0.7 copy-start.3
  27.2 0.7 copy-start.4
  27.9 0.7 copy-start.5
  51.7 1.0 copy-start.6
  60.1 57.8 %all-to-all-start.1 = ((f32[16,256,128]{2,1,0:T(8,128)}), f32[16,256,128]{2,1,0:T(8,128)}, u32[]{:S(2)}, u32[]{:S(2)}) async-start(f32[16,256,128]{2,1,0:T(8,128)} %bitcast.31), calls=%async_computation.1 | async-start | bytes 4194304 | tf_op jit(solution)/shard_map/all_to_all | solution.py:410

commit v2 on v1

--- a/solution.py
+++ b/solution.py
@@ -28,14 +28,18 @@
     adj_ref,
     fwd_ref,
     logc_ref,
-    spacing_ref,
-    residual_ref,
+    spacing_hbm,
+    residual_hbm,
     gate_ref,
-    counts_ref,
-    model_ref,
+    counts_hbm,
+    model_hbm,
     out_ref,
     sens_ref,
     reg_ref,
+    spacing_ref,
+    residual_ref,
+    counts_ref,
+    model_ref,
     field,
     curl,
     coef,
@@ -60,13 +64,26 @@
 ):
     steps = fwd_ref.shape[0]
     cells, ny, nz = logc_ref.shape
-    rows_v = model_ref.shape[0]
+    rows_v = model_hbm.shape[0]
     grp, me = lax.axis_index("grp"), lax.axis_index("tx")
     low, high = lax.rem(me + n - 1, n), lax.rem(me + 1, n)
     has_low, has_high = me > 0, me < n - 1
     chunk = 64
     chunks = [(y, chunk) for y in range(0, ny, chunk)]
 
+    small = [
+        pltpu.make_async_copy(source, target, local_sem.at[6 + i])
+        for i, (source, target) in enumerate(
+            (
+                (spacing_hbm, spacing_ref),
+                (counts_hbm, counts_ref),
+                (residual_hbm, residual_ref),
+                (model_hbm, model_ref),
+            )
+        )
+    ]
+    for copy in small[:3]:
+        copy.start()
     load_last = pltpu.make_async_copy(
         adj_ref.at[:, pl.ds(cells - 1, 1)], field.at[:, pl.ds(cells - 1, 1), pl.ds(0, ny)], local_sem.at[0]
     )
@@ -80,11 +97,14 @@
     load_terms = [pltpu.make_async_copy(fwd_ref.at[s], terms.at[s], term_sem.at[s]) for s in range(steps)]
     for copy in load_terms:
         copy.start()
+    small[3].start()
 
     barrier = pltpu.get_barrier_semaphore()
     for neighbour in (low, high):
         pl.semaphore_signal(barrier, inc=1, device_id=(grp, neighbour), device_id_type=MESH)
 
+    for copy in small[:3]:
+        copy.wait()
     inverse = 1.0 / spacing_ref[...]
     depth_count = counts_ref[...].astype(jnp.float32)
     sources = [residual_ref[gate_ref[s]] for s in range(steps)]
@@ -181,7 +201,7 @@
 
     def model_up():
         return pltpu.make_async_remote_copy(
-            src_ref=model_ref.at[rows_v - 1],
+            src_ref=model_hbm.at[rows_v - 1],
             dst_ref=model_low,
             send_sem=model_send.at[0],
             recv_sem=model_recv.at[0],
@@ -191,7 +211,7 @@
 
     def model_down():
         return pltpu.make_async_remote_copy(
-            src_ref=model_ref.at[0],
+            src_ref=model_hbm.at[0],
             dst_ref=model_high,
             send_sem=model_send.at[1],
             recv_sem=model_recv.at[1],
@@ -236,6 +256,7 @@
             model_down().wait_send()
             model_up().wait_recv()
 
+        small[3].wait()
         for v in range(rows_v):
             model[v, pl.ds(0, 8), :] = jnp.zeros((8, nz), jnp.float32)
             model[v, pl.ds(ny + 8, 8), :] = jnp.zeros((8, nz), jnp.float32)
@@ -320,7 +341,10 @@
         inside = lane_index((ny, nz)).astype(jnp.float32) < jnp.broadcast_to(
             columns[:, cells + x : cells + x + 1], (ny, nz)
         )
-        sens_ref[x] = jnp.where(inside, -0.7 * coef[x] * total[x], 0.0)
+        sens = jnp.where(inside, -0.7 * coef[x] * total[x], 0.0)
+        coarse = sens.astype(jnp.bfloat16)
+        sens_ref[x, :, 0:nz] = coarse
+        sens_ref[x, :, nz : 2 * nz] = (sens - coarse.astype(jnp.float32)).astype(jnp.bfloat16)
     store(1, cells - 2, 3).wait()
     store(0, 1, 4).wait()
     store(cells - 1, 1, 5).wait()
@@ -336,12 +360,16 @@
         functools.partial(field_kernel, n),
         out_shape=(
             jax.ShapeDtypeStruct(adj.shape, f32),
-            jax.ShapeDtypeStruct(logc.shape, f32),
+            jax.ShapeDtypeStruct((cells, ny, 2 * nz), jnp.bfloat16),
             jax.ShapeDtypeStruct(model.shape, f32),
         ),
-        in_specs=[anywhere] * 3 + [vmem, vmem, pl.BlockSpec(memory_space=pltpu.SMEM), vmem, vmem],
+        in_specs=[anywhere] * 5 + [pl.BlockSpec(memory_space=pltpu.SMEM), anywhere, anywhere],
         out_specs=(anywhere, vmem, vmem),
         scratch_shapes=[
+            pltpu.VMEM(spacing.shape, f32),
+            pltpu.VMEM(residuals.shape, f32),
+            pltpu.VMEM(counts.shape, jnp.int32),
+            pltpu.VMEM(model.shape, f32),
             pltpu.VMEM((3, cells, ny + 8, nz), f32),
             pltpu.VMEM((3, cells + 1, ny + 8, nz), f32),
             pltpu.VMEM((cells, ny, nz), f32),
@@ -355,7 +383,7 @@
             pltpu.VMEM((model.shape[0], ny + 16, nz), f32),
             pltpu.VMEM((ny, nz), f32),
             pltpu.VMEM((ny, nz), f32),
-            dma((6,)),
+            dma((10,)),
             dma((steps,)),
             dma((steps,)),
             dma((steps,)),
@@ -366,6 +394,229 @@
         ],
         compiler_params=pltpu.CompilerParams(collective_id=0, has_side_effects=True, vmem_limit_bytes=48 << 20),
     )(adj, fwd, logc, spacing, residuals, gates, counts, model)
+
+
+def relayout_kernel(
+    n,
+    sens_hbm,
+    voxel_hbm,
+    reg_hbm,
+    out_ref,
+    sens,
+    voxel,
+    ids,
+    reg,
+    to_pair,
+    from_pair,
+    across,
+    from_across,
+    held,
+    arrived,
+    load_sem,
+    pair_send,
+    pair_recv,
+    across_send,
+    across_recv,
+    layer_send,
+    layer_recv,
+):
+    layers = n // 4
+    cells, ny = voxel_hbm.shape
+    voxels, nz = reg_hbm.shape
+    grp, me = lax.axis_index("grp"), lax.axis_index("tx")
+    core, half, layer = lax.rem(me, 2), lax.rem(me // 2, 2), me // 4
+    up = jnp.where(layer < layers // 2, 1, 0)
+
+    def tile(z, y, c):
+        return (z * 2 + y) * 2 + c
+
+    def layer_at(k):
+        return up * (layers - 1 - k) + (1 - up) * k
+
+    loads = [
+        pltpu.make_async_copy(source, target, load_sem.at[i])
+        for i, (source, target) in enumerate(((sens_hbm, sens), (voxel_hbm, voxel), (reg_hbm, reg)))
+    ]
+    for copy in loads:
+        copy.start()
+    barrier = pltpu.get_barrier_semaphore()
+    for other in (tile(layer, half, 1 - core), tile(layer, 1 - half, core)):
+        pl.semaphore_signal(barrier, inc=1, device_id=(grp, other), device_id_type=MESH)
+
+    def greet(z, carry):
+        @pl.when(z != layer)
+        def _():
+            pl.semaphore_signal(
+                barrier, inc=1, device_id=(grp, tile(z, half, core)), device_id_type=MESH
+            )
+
+        return carry
+
+    lax.fori_loop(0, layers, greet, 0)
+    for copy in loads:
+        copy.wait()
+    for x in range(cells):
+        ids[:, x * ny : (x + 1) * ny] = voxel[x : x + 1, :]
+
+    def pair_copy(k, y):
+        return pltpu.make_async_remote_copy(
+            src_ref=to_pair.at[k, y],
+            dst_ref=from_pair.at[k, y],
+            send_sem=pair_send.at[k, y],
+            recv_sem=pair_recv.at[k, y],
+            device_id=(grp, tile(layer, half, 1 - core)),
+            device_id_type=MESH,
+        )
+
+    def across_copy(k):
+        return pltpu.make_async_remote_copy(
+            src_ref=across.at[k],
+            dst_ref=from_across.at[k],
+            send_sem=across_send.at[k],
+            recv_sem=across_recv.at[k],
+            device_id=(grp, tile(layer, 1 - half, core)),
+            device_id_type=MESH,
+        )
+
+    def layer_copy(k):
+        return pltpu.make_async_remote_copy(
+            src_ref=held.at[k],
+            dst_ref=arrived.at[layer],
+            send_sem=layer_send.at[k],
+            recv_sem=layer_recv.at[layer],
+            device_id=(grp, tile(layer_at(k), half, core)),
+            device_id_type=MESH,
+        )
+
+    def arrival(z):
+        return pltpu.make_async_remote_copy(
+            src_ref=held.at[0],
+            dst_ref=arrived.at[z],
+            send_sem=layer_send.at[0],
+            recv_sem=layer_recv.at[z],
+            device_id=(grp, tile(z, half, core)),
+            device_id_type=MESH,
+        )
+
+    size = 256
+
+    def partial_sums(target, put):
+        for first in range(0, voxels, size):
+            wanted = lax.broadcasted_iota(jnp.int32, (size, cells * ny), 0)
+            here = wanted == ids[...] - (target * voxels + first)
+            picked = jnp.where(here, 1.0, 0.0).astype(jnp.bfloat16)
+            sums = jnp.dot(picked, sens[...], preferred_element_type=jnp.float32)
+            put(pl.ds(first, size), sums[:, 0:nz] + sums[:, nz : 2 * nz])
+
+    def forward(k):
+        across_copy(k).wait_recv()
+        pair_copy(k, 1).wait_recv()
+        held[k] = held[k] + from_pair[k, 1] + from_across[k]
+
+        @pl.when(layer_at(k) != layer)
+        def _():
+            layer_copy(k).start()
+
+    def stage(k, carry):
+        z = layer_at(k)
+
+        def put_pair(y):
+            def put(at, value):
+                to_pair[k, y, at, :] = value
+
+            return put
+
+        def put_across(at, value):
+            across[k, at, :] = value
+
+        def put_held(at, value):
+            held[k, at, :] = value
+
+        partial_sums(tile(z, 1 - half, 1 - core), put_pair(0))
+
+        @pl.when(k == 0)
+        def _():
+            pl.semaphore_wait(barrier, layers + 1)
+
+        pair_copy(k, 0).start()
+        partial_sums(tile(z, 1 - half, core), put_across)
+        pair_copy(k, 0).wait_recv()
+        across[k] = across[k] + from_pair[k, 0]
+        across_copy(k).start()
+        partial_sums(tile(z, half, 1 - core), put_pair(1))
+        pair_copy(k, 1).start()
+        partial_sums(tile(z, half, core), put_held)
+
+        @pl.when(k > 0)
+        def _():
+            forward(k - 1)
+
+        return carry
+
+    lax.fori_loop(0, layers, stage, 0)
+    forward(layers - 1)
+    own = up * (layers - 1 - layer) + (1 - up) * layer
+    out_ref[...] = reg[...] + held[own]
+
+    def collect(z, carry):
+        @pl.when(z != layer)
+        def _():
+            arrival(z).wait_recv()
+            out_ref[...] = out_ref[...] + arrived[z]
+
+        return carry
+
+    lax.fori_loop(0, layers, collect, 0)
+
+    def drain(k, carry):
+        pair_copy(k, 0).wait_send()
+        pair_copy(k, 1).wait_send()
+        across_copy(k).wait_send()
+
+        @pl.when(layer_at(k) != layer)
+        def _():
+            layer_copy(k).wait_send()
+
+        return carry
+
+    lax.fori_loop(0, layers, drain, 0)
+
+
+def relayout(n, sensitivity, voxel_column, regularity):
+    cells, ny = voxel_column.shape
+    nz = regularity.shape[2]
+    voxels = regularity.shape[0] * regularity.shape[1]
+    layers = n // 4
+    f32, dma = jnp.float32, pltpu.SemaphoreType.DMA
+    anywhere = pl.BlockSpec(memory_space=pl.ANY)
+    block = (voxels, nz)
+    out = pl.pallas_call(
+        functools.partial(relayout_kernel, n),
+        out_shape=jax.ShapeDtypeStruct(block, f32),
+        in_specs=[anywhere] * 3,
+        out_specs=pl.BlockSpec(memory_space=pltpu.VMEM),
+        scratch_shapes=[
+            pltpu.VMEM((cells * ny, 2 * nz), jnp.bfloat16),
+            pltpu.VMEM((cells, ny), jnp.int32),
+            pltpu.VMEM((1, cells * ny), jnp.int32),
+            pltpu.VMEM(block, f32),
+            pltpu.VMEM((layers, 2) + block, f32),
+            pltpu.VMEM((layers, 2) + block, f32),
+            pltpu.VMEM((layers,) + block, f32),
+            pltpu.VMEM((layers,) + block, f32),
+            pltpu.VMEM((layers,) + block, f32),
+            pltpu.VMEM((layers,) + block, f32),
+            dma((3,)),
+            dma((layers, 2)),
+            dma((layers, 2)),
+            dma((layers,)),
+            dma((layers,)),
+            dma((layers,)),
+            dma((layers,)),
+        ],
+        compiler_params=pltpu.CompilerParams(collective_id=1, has_side_effects=True, vmem_limit_bytes=52 << 20),
+    )(sensitivity.reshape(cells * ny, 2 * nz), voxel_column, regularity.reshape(block))
+    return out.reshape(regularity.shape)
 
 
 def body(
@@ -379,7 +630,6 @@
     voxel_column,
     voxel_model,
 ):
-    depth = adjoint_in.shape[3]
     tile_count = lax.axis_size("tx")
     adjoint, sensitivity, regularity = field_phase(
         tile_count,
@@ -392,42 +642,8 @@
         counts,
         voxel_model,
     )
-    column_count = counts.shape[0] * counts.shape[1]
-    capacity = 2 * column_count // tile_count
-    voxel_count = voxel_model.shape[0] * voxel_model.shape[1]
-    columns = sensitivity.reshape(column_count, depth)
-    voxel_ids = voxel_column.reshape(column_count)
-    target = voxel_ids // voxel_count
-    local_voxel = voxel_ids % voxel_count
-    one_hot = (target[:, None] == jnp.arange(tile_count, dtype=jnp.int32)[None, :]).astype(
-        jnp.int32
-    )
-    slot_rank = jnp.sum((jnp.cumsum(one_hot, axis=0) - 1) * one_hot, axis=1)
-    position = target * capacity + slot_rank
-    send_rows = jnp.zeros((tile_count * capacity, depth), jnp.float32).at[position].set(columns)
-    send_ids = jnp.full((tile_count * capacity,), -1, jnp.int32).at[position].set(local_voxel)
-    received, received_ids = (
-        lax.all_to_all(
-            send_rows.reshape(tile_count, capacity, depth),
-            "tx",
-            split_axis=0,
-            concat_axis=0,
-            tiled=True,
-        ),
-        lax.all_to_all(
-            send_ids.reshape(tile_count, capacity), "tx", split_axis=0, concat_axis=0, tiled=True
-        ),
-    )
-    received = received.reshape(tile_count * capacity, depth)
-    received_ids = received_ids.reshape(tile_count * capacity)
-    selector = (jnp.arange(voxel_count, dtype=jnp.int32)[:, None] == received_ids[None, :]).astype(
-        jnp.float32
-    )
-    collected = jnp.dot(
-        selector, received, precision=lax.Precision.HIGHEST, preferred_element_type=jnp.float32
-    )
-    collected = collected.reshape(voxel_model.shape)
-    return (adjoint, collected + regularity)
+    gradient = relayout(tile_count, sensitivity, voxel_column, regularity)
+    return (adjoint, gradient)
 
 
 def solution(mesh):

time: 126 us -> 75.5 us (0.60)
  the two profiles are of different devices: /device:TPU:15 before, /device:TPU:0 now
where the time goes in v2:
time: 75.5 us; the launch traced here: 75.2 us
  Pallas kernels  67 us (89%)
  local copies, waits for them, and re-layouts  7.55 us (10%)
    pallas_call x1, Pallas kernels, relayout(): pl.pallas_call(functools.partial(relayout_kernel, n), out_shape=jax.Shape...  45.4 us
    pallas_call x1, Pallas kernels, field_phase(): pl.pallas_call(functools.partial(field_kernel, n), out_shape=(jax.ShapeDt...  21.6 us
    unnamed x16, local copies, waits for them, and re-layouts  7.55 us

profile of v2, /device:TPU:0, one launch (start us, length us, event | category | flops | bytes accessed | tf_op | source)
XLA Modules:
  0.0 75.2 jit_solution(13950246859287136065)
XLA Ops:
  0.6 0.0 copy-start
  0.6 1.2 %copy-done = f32[8,256,128]{2,1,0:T(8,128)S(1)} copy-done((f32[8,256,128]{2,1,0:T(8,128)S(1)}, f32[8,256,128]{2,1,0:T(8,128)}, u32[]{:S(2)}) %copy-start) | copy-done | bytes 1048600
  1.9 0.0 copy-start.1
  1.9 1.0 %copy-done.1 = f32[35,8,256]{2,1,0:T(8,128)S(1)} copy-done((f32[35,8,256]{2,1,0:T(8,128)S(1)}, f32[35,8,256]{2,1,0:T(8,128)}, u32[]{:S(2)}) %copy-start.1) | copy-done | bytes 286744
  2.8 0.0 copy-start.2
  2.8 0.9 %copy-done.2 = f32[2,256,128]{2,1,0:T(8,128)S(1)} copy-done((f32[2,256,128]{2,1,0:T(8,128)S(1)}, f32[2,256,128]{2,1,0:T(8,128)}, u32[]{:S(2)}) %copy-start.2) | copy-done | bytes 262168
  3.8 0.0 copy-start.4
  3.8 0.7 copy-done.4
  4.5 0.0 copy-start.5
  4.5 0.7 copy-done.5
  5.2 0.0 copy-start.6
  5.2 0.7 copy-done.6
  5.8 0.0 copy-start.3
  5.8 21.6 %shard_map.104 = (f32[3,8,256,128]{3,2,1,0:T(8,128)S(1)}, bf16[8,256,256]{2,1,0:T(8,128)(2,1)S(1)}, f32[2,256,128]{2,1,0:T(8,128)S(1)}) custom-call(f32[3,8,256,128]{3,2,1,0:T(8,128)} %adj_ref.1, bf16[3,3,8,256,128]{4,3,2,1,0:T(8,128)(2,1)} %fwd_ref.1, f32[8,256,128]{2,1,0:T(8,128)S(1)} %copy-done, f32[8,256]{1,0:T(8,128)S(1)} %copy-done.4, ...), custom_call_target="tpu_custom_call" | custom-call | tf_op jit(solution)/shard_map/pallas_call | solution.py:359
  27.4 0.0 copy-done.3
  27.4 45.4 %shard_map.105 = f32[512,128]{1,0:T(8,128)S(1)} custom-call(bf16[2048,256]{1,0:T(8,128)(2,1)S(1)} %bitcast.3, s32[8,256]{1,0:T(8,128)S(1)} %copy-done.3, f32[512,128]{1,0:T(8,128)S(1)} %bitcast.5), custom_call_target="tpu_custom_call" | custom-call | tf_op jit(solution)/shard_map/pallas_call | solution.py:593
  72.8 1.7 %copy.13 = f32[3,8,256,128]{3,2,1,0:T(8,128)} copy(f32[3,8,256,128]{3,2,1,0:T(8,128)S(1)} %get-tuple-element.10) | data formatting | bytes 6291456
  74.5 0.7 copy.14
Async XLA Ops:
  0.6 1.2 %copy-start = (f32[8,256,128]{2,1,0:T(8,128)S(1)}, f32[8,256,128]{2,1,0:T(8,128)}, u32[]{:S(2)}) copy-start(f32[8,256,128]{2,1,0:T(8,128)} %logc_ref.1) | copy-start | bytes 3145732
  1.9 1.0 %copy-start.1 = (f32[35,8,256]{2,1,0:T(8,128)S(1)}, f32[35,8,256]{2,1,0:T(8,128)}, u32[]{:S(2)}) copy-start(f32[35,8,256]{2,1,0:T(8,128)} %residual_hbm.1) | copy-start | bytes 860164
  2.8 0.9 %copy-start.2 = (f32[2,256,128]{2,1,0:T(8,128)S(1)}, f32[2,256,128]{2,1,0:T(8,128)}, u32[]{:S(2)}) copy-start(f32[2,256,128]{2,1,0:T(8,128)} %model_hbm.1) | copy-start | bytes 786436
  3.8 0.7 copy-start.4
  4.5 0.7 copy-start.5
  5.2 0.7 copy-start.6
  5.8 21.6 %copy-start.3 = (s32[8,256]{1,0:T(8,128)S(1)}, s32[8,256]{1,0:T(8,128)}, u32[]{:S(2)}) copy-start(s32[8,256]{1,0:T(8,128)} %voxel_hbm.1) | copy-start | bytes 24580

commit v3 on v2

--- a/solution.py
+++ b/solution.py
@@ -354,7 +354,7 @@
     steps = fwd.shape[0]
     cells, ny, nz = logc.shape
     f32 = jnp.float32
-    anywhere, vmem = pl.BlockSpec(memory_space=pl.ANY), pl.BlockSpec(memory_space=pltpu.VMEM)
+    anywhere, far, vmem = pl.BlockSpec(memory_space=pl.ANY), pl.BlockSpec(memory_space=pltpu.HBM), pl.BlockSpec(memory_space=pltpu.VMEM)
     dma = pltpu.SemaphoreType.DMA
     return pl.pallas_call(
         functools.partial(field_kernel, n),
@@ -363,7 +363,7 @@
             jax.ShapeDtypeStruct((cells, ny, 2 * nz), jnp.bfloat16),
             jax.ShapeDtypeStruct(model.shape, f32),
         ),
-        in_specs=[anywhere] * 5 + [pl.BlockSpec(memory_space=pltpu.SMEM), anywhere, anywhere],
+        in_specs=[far] * 5 + [pl.BlockSpec(memory_space=pltpu.SMEM), far, far],
         out_specs=(anywhere, vmem, vmem),
         scratch_shapes=[
             pltpu.VMEM(spacing.shape, f32),
@@ -392,7 +392,7 @@
             dma((2,)),
             dma((2,)),
         ],
-        compiler_params=pltpu.CompilerParams(collective_id=0, has_side_effects=True, vmem_limit_bytes=48 << 20),
+        compiler_params=pltpu.CompilerParams(collective_id=0, has_side_effects=True, vmem_limit_bytes=60 << 20),
     )(adj, fwd, logc, spacing, residuals, gates, counts, model)
 
 
@@ -423,6 +423,7 @@
     layers = n // 4
     cells, ny = voxel_hbm.shape
     voxels, nz = reg_hbm.shape
+    blocks, size = 2 * layers, voxels // 2
     grp, me = lax.axis_index("grp"), lax.axis_index("tx")
     core, half, layer = lax.rem(me, 2), lax.rem(me // 2, 2), me // 4
     up = jnp.where(layer < layers // 2, 1, 0)
@@ -481,71 +482,53 @@
     def layer_copy(k):
         return pltpu.make_async_remote_copy(
             src_ref=held.at[k],
-            dst_ref=arrived.at[layer],
+            dst_ref=arrived.at[layer, lax.rem(k, 2)],
             send_sem=layer_send.at[k],
-            recv_sem=layer_recv.at[layer],
-            device_id=(grp, tile(layer_at(k), half, core)),
-            device_id_type=MESH,
-        )
-
-    def arrival(z):
+            recv_sem=layer_recv.at[layer, lax.rem(k, 2)],
+            device_id=(grp, tile(layer_at(k // 2), half, core)),
+            device_id_type=MESH,
+        )
+
+    def arrival(z, part):
         return pltpu.make_async_remote_copy(
             src_ref=held.at[0],
-            dst_ref=arrived.at[z],
+            dst_ref=arrived.at[z, part],
             send_sem=layer_send.at[0],
-            recv_sem=layer_recv.at[z],
+            recv_sem=layer_recv.at[z, part],
             device_id=(grp, tile(z, half, core)),
             device_id_type=MESH,
         )
 
-    size = 256
-
-    def partial_sums(target, put):
-        for first in range(0, voxels, size):
-            wanted = lax.broadcasted_iota(jnp.int32, (size, cells * ny), 0)
-            here = wanted == ids[...] - (target * voxels + first)
-            picked = jnp.where(here, 1.0, 0.0).astype(jnp.bfloat16)
-            sums = jnp.dot(picked, sens[...], preferred_element_type=jnp.float32)
-            put(pl.ds(first, size), sums[:, 0:nz] + sums[:, nz : 2 * nz])
+    def target_sums(k, y, c):
+        first = tile(layer_at(k // 2), y, c) * voxels + lax.rem(k, 2) * size
+        here = lax.broadcasted_iota(jnp.int32, (size, cells * ny), 0) == ids[...] - first
+        picked = jnp.where(here, 1.0, 0.0).astype(jnp.bfloat16)
+        sums = jnp.dot(picked, sens[...], preferred_element_type=jnp.float32)
+        return sums[:, 0:nz] + sums[:, nz : 2 * nz]
 
     def forward(k):
         across_copy(k).wait_recv()
         pair_copy(k, 1).wait_recv()
         held[k] = held[k] + from_pair[k, 1] + from_across[k]
 
-        @pl.when(layer_at(k) != layer)
+        @pl.when(layer_at(k // 2) != layer)
         def _():
             layer_copy(k).start()
 
     def stage(k, carry):
-        z = layer_at(k)
-
-        def put_pair(y):
-            def put(at, value):
-                to_pair[k, y, at, :] = value
-
-            return put
-
-        def put_across(at, value):
-            across[k, at, :] = value
-
-        def put_held(at, value):
-            held[k, at, :] = value
-
-        partial_sums(tile(z, 1 - half, 1 - core), put_pair(0))
-
-        @pl.when(k == 0)
-        def _():
-            pl.semaphore_wait(barrier, layers + 1)
-
-        pair_copy(k, 0).start()
-        partial_sums(tile(z, 1 - half, core), put_across)
+        across[k] = target_sums(k, 1 - half, core)
         pair_copy(k, 0).wait_recv()
         across[k] = across[k] + from_pair[k, 0]
         across_copy(k).start()
-        partial_sums(tile(z, half, 1 - core), put_pair(1))
+
+        @pl.when(k < blocks - 1)
+        def _():
+            to_pair[k + 1, 0] = target_sums(k + 1, 1 - half, 1 - core)
+            pair_copy(k + 1, 0).start()
+
+        to_pair[k, 1] = target_sums(k, half, 1 - core)
         pair_copy(k, 1).start()
-        partial_sums(tile(z, half, core), put_held)
+        held[k] = target_sums(k, half, core)
 
         @pl.when(k > 0)
         def _():
@@ -553,16 +536,23 @@
 
         return carry
 
-    lax.fori_loop(0, layers, stage, 0)
-    forward(layers - 1)
+    to_pair[0, 0] = target_sums(0, 1 - half, 1 - core)
+    pl.semaphore_wait(barrier, layers + 1)
+    pair_copy(0, 0).start()
+    lax.fori_loop(0, blocks, stage, 0)
+    forward(blocks - 1)
     own = up * (layers - 1 - layer) + (1 - up) * layer
-    out_ref[...] = reg[...] + held[own]
+    for part in range(2):
+        at = pl.ds(part * size, size)
+        out_ref[at, :] = reg[at, :] + held[2 * own + part]
 
     def collect(z, carry):
         @pl.when(z != layer)
         def _():
-            arrival(z).wait_recv()
-            out_ref[...] = out_ref[...] + arrived[z]
+            for part in range(2):
+                at = pl.ds(part * size, size)
+                arrival(z, part).wait_recv()
+                out_ref[at, :] = out_ref[at, :] + arrived[z, part]
 
         return carry
 
@@ -573,13 +563,13 @@
         pair_copy(k, 1).wait_send()
         across_copy(k).wait_send()
 
-        @pl.when(layer_at(k) != layer)
+        @pl.when(layer_at(k // 2) != layer)
         def _():
             layer_copy(k).wait_send()
 
         return carry
 
-    lax.fori_loop(0, layers, drain, 0)
+    lax.fori_loop(0, blocks, drain, 0)
 
 
 def relayout(n, sensitivity, voxel_column, regularity):
@@ -588,33 +578,34 @@
     voxels = regularity.shape[0] * regularity.shape[1]
     layers = n // 4
     f32, dma = jnp.float32, pltpu.SemaphoreType.DMA
-    anywhere = pl.BlockSpec(memory_space=pl.ANY)
-    block = (voxels, nz)
+    far = pl.BlockSpec(memory_space=pltpu.HBM)
+    block, part = (voxels, nz), (voxels // 2, nz)
+    blocks = 2 * layers
     out = pl.pallas_call(
         functools.partial(relayout_kernel, n),
         out_shape=jax.ShapeDtypeStruct(block, f32),
-        in_specs=[anywhere] * 3,
+        in_specs=[far] * 3,
         out_specs=pl.BlockSpec(memory_space=pltpu.VMEM),
         scratch_shapes=[
             pltpu.VMEM((cells * ny, 2 * nz), jnp.bfloat16),
             pltpu.VMEM((cells, ny), jnp.int32),
             pltpu.VMEM((1, cells * ny), jnp.int32),
             pltpu.VMEM(block, f32),
-            pltpu.VMEM((layers, 2) + block, f32),
-            pltpu.VMEM((layers, 2) + block, f32),
-            pltpu.VMEM((layers,) + block, f32),
-            pltpu.VMEM((layers,) + block, f32),
-            pltpu.VMEM((layers,) + block, f32),
-            pltpu.VMEM((layers,) + block, f32),
+            pltpu.VMEM((blocks, 2) + part, f32),
+            pltpu.VMEM((blocks, 2) + part, f32),
+            pltpu.VMEM((blocks,) + part, f32),
+            pltpu.VMEM((blocks,) + part, f32),
+            pltpu.VMEM((blocks,) + part, f32),
+            pltpu.VMEM((layers, 2) + part, f32),
             dma((3,)),
+            dma((blocks, 2)),
+            dma((blocks, 2)),
+            dma((blocks,)),
+            dma((blocks,)),
+            dma((blocks,)),
             dma((layers, 2)),
-            dma((layers, 2)),
-            dma((layers,)),
-            dma((layers,)),
-            dma((layers,)),
-            dma((layers,)),
         ],
-        compiler_params=pltpu.CompilerParams(collective_id=1, has_side_effects=True, vmem_limit_bytes=52 << 20),
+        compiler_params=pltpu.CompilerParams(collective_id=1, has_side_effects=True, vmem_limit_bytes=60 << 20),
     )(sensitivity.reshape(cells * ny, 2 * nz), voxel_column, regularity.reshape(block))
     return out.reshape(regularity.shape)
 

time: 75.5 us -> 71.7 us (0.950)
  local copies, waits for them, and re-layouts: 7.55 us -> 4.61 us
  Pallas kernels: 67 us -> 66.2 us
    unnamed x16 -> x4, local copies, waits for them, and re-layouts: 7.55 us -> 4.61 us
    pallas_call x1, Pallas kernels: 45.4 us -> 43.4 us  [relayout(): pl.pallas_call(functools.partial(relayout_kernel, n), out_shape=jax.Shape...]
    pallas_call x1, Pallas kernels: 21.6 us -> 22.8 us  [field_phase(): pl.pallas_call(functools.partial(field_kernel, n), out_shape=(jax.ShapeDt...]
where the time goes in v3:
time: 71.7 us; the launch traced here: 71.5 us
  Pallas kernels  66.2 us (92%)
  local copies, waits for them, and re-layouts  4.61 us (6%)
    pallas_call x1, Pallas kernels, relayout(): pl.pallas_call(functools.partial(relayout_kernel, n), out_shape=jax.Shape...  43.4 us
    pallas_call x1, Pallas kernels, field_phase(): pl.pallas_call(functools.partial(field_kernel, n), out_shape=(jax.ShapeDt...  22.8 us
    unnamed x4, local copies, waits for them, and re-layouts  4.61 us

profile of v3, /device:TPU:0, one launch (start us, length us, event | category | flops | bytes accessed | tf_op | source)
XLA Modules:
  0.0 71.5 jit_solution(4331053271921912874)
XLA Ops:
  0.6 22.8 %shard_map.104 = (f32[3,8,256,128]{3,2,1,0:T(8,128)}, bf16[8,256,256]{2,1,0:T(8,128)(2,1)}, f32[2,256,128]{2,1,0:T(8,128)}) custom-call(f32[3,8,256,128]{3,2,1,0:T(8,128)} %adj_ref.1, bf16[3,3,8,256,128]{4,3,2,1,0:T(8,128)(2,1)} %fwd_ref.1, f32[8,256,128]{2,1,0:T(8,128)} %logc_ref.1, f32[8,256]{1,0:T(8,128)} %spacing_hbm.1, f32[35,8,256]{2,1,0:T(8,128)} %residual_hbm.1, ...), custom_call_target="tpu_custom_call" | custom-call | tf_op jit(solution)/shard_map/pallas_call | solution.py:359
  23.4 43.4 %shard_map.105 = f32[512,128]{1,0:T(8,128)} custom-call(bf16[2048,256]{1,0:T(8,128)(2,1)} %bitcast.3, s32[8,256]{1,0:T(8,128)} %voxel_hbm.1, f32[512,128]{1,0:T(8,128)} %bitcast.5), custom_call_target="tpu_custom_call" | custom-call | tf_op jit(solution)/shard_map/pallas_call | solution.py:584
  66.8 0.0 copy-start
  66.9 3.9 %copy.13 = f32[3,8,256,128]{3,2,1,0:T(8,128)} copy(f32[3,8,256,128]{3,2,1,0:T(8,128)} %get-tuple-element.10) | data formatting | bytes 6291456
  70.8 0.0 copy-done
  70.8 0.7 copy.14
Async XLA Ops:
  66.8 3.9 %copy-start = (f32[512,128]{1,0:T(8,128)S(1)}, f32[512,128]{1,0:T(8,128)}, u32[]{:S(2)}) copy-start(f32[512,128]{1,0:T(8,128)} %shard_map.105) | copy-start | bytes 786436

commit v4 on v3

--- a/solution.py
+++ b/solution.py
@@ -69,7 +69,16 @@
     low, high = lax.rem(me + n - 1, n), lax.rem(me + 1, n)
     has_low, has_high = me > 0, me < n - 1
     chunk = 64
-    chunks = [(y, chunk) for y in range(0, ny, chunk)]
+
+
+    def pieces(first, last):
+        return [(y, min(chunk, last - y)) for y in range(first, last, chunk)]
+
+    chunks = pieces(0, ny)
+
+    def halves(slot):
+        middle = ny // 2 + 8 * (1 - slot)
+        return ((0, middle), (middle, ny))
 
     small = [
         pltpu.make_async_copy(source, target, local_sem.at[6 + i])
@@ -119,29 +128,34 @@
             field[a, x, pl.ds(ny, 8), :] = jnp.zeros((8, nz), jnp.float32)
             curl[a, x + 1, pl.ds(0, 8), :] = jnp.zeros((8, nz), jnp.float32)
 
-    def copy_up(slot):
-        return pltpu.make_async_remote_copy(
-            src_ref=to_high.at[slot],
-            dst_ref=from_low.at[slot],
-            send_sem=send_up.at[slot],
-            recv_sem=recv_low.at[slot],
+    def copy_up(slot, part):
+        first, last = halves(slot)[part]
+        at = pl.ds(first, last - first)
+        return pltpu.make_async_remote_copy(
+            src_ref=to_high.at[slot, :, at],
+            dst_ref=from_low.at[slot, :, at],
+            send_sem=send_up.at[slot, part],
+            recv_sem=recv_low.at[slot, part],
             device_id=(grp, high),
             device_id_type=MESH,
         )
 
-    def copy_down(slot):
-        return pltpu.make_async_remote_copy(
-            src_ref=field.at[pl.ds(1, 2), 0, pl.ds(0, ny)],
-            dst_ref=from_high.at[slot],
-            send_sem=send_down.at[slot],
-            recv_sem=recv_high.at[slot],
+    def copy_down(slot, part):
+        first, last = halves(slot)[part]
+        at = pl.ds(first, last - first)
+        origin = adj_ref if slot == 0 else field
+        return pltpu.make_async_remote_copy(
+            src_ref=origin.at[pl.ds(1, 2), 0, at],
+            dst_ref=from_high.at[slot, :, at],
+            send_sem=send_down.at[slot, part],
+            recv_sem=recv_high.at[slot, part],
             device_id=(grp, low),
             device_id_type=MESH,
         )
 
-    def send_high(slot):
+    def send_high(slot, part):
         x = cells - 1
-        for y, size in chunks:
+        for y, size in pieces(*halves(slot)[part]):
             e0, e1, e2 = (field[a, x, pl.ds(y, size), :] for a in range(3))
             e0y = field[0, x, pl.ds(y + 1, size), :]
             to_high[slot, 0, pl.ds(y, size), :] = inv[x, pl.ds(y, size), :] * (next_z(e0) - e0) + e2
@@ -149,15 +163,15 @@
 
         @pl.when(has_high)
         def _():
-            copy_up(slot).start()
-
-    def send_low(slot):
+            copy_up(slot, part).start()
+
+    def send_low(slot, part):
         @pl.when(has_low)
         def _():
-            copy_down(slot).start()
-
-    def curl_row(x, next_row):
-        for y, size in chunks:
+            copy_down(slot, part).start()
+
+    def curl_row(x, next_row, where=chunks):
+        for y, size in where:
             at = pl.ds(y, size)
             e0, e1, e2 = (field[a, x, at, :] for a in range(3))
             e0y, e2y = field[0, x, pl.ds(y + 1, size), :], field[2, x, pl.ds(y + 1, size), :]
@@ -168,8 +182,8 @@
             curl[1, x + 1, to, :] = h * (next_z(e0) - e0) - (e2x - e2)
             curl[2, x + 1, to, :] = (e1x - e1) - (e0y - e0)
 
-    def update_row(s, x):
-        for y, size in chunks:
+    def update_row(s, x, where=chunks):
+        for y, size in where:
             at, to, before = pl.ds(y, size), pl.ds(y + 8, size), pl.ds(y + 7, size)
             h, c = inv[x, at, :], coef[x, at, :]
             h0, h1, h2 = (curl[a, x + 1, to, :] for a in range(3))
@@ -194,10 +208,12 @@
             total[x, at, :] = value if s == 0 else total[x, at, :] + value
 
     pl.semaphore_wait(barrier, 2)
+    send_low(0, 0)
     load_last.wait()
-    send_high(0)
+    send_high(0, 0)
+    send_low(0, 1)
+    send_high(0, 1)
     load_rest.wait()
-    send_low(0)
 
     def model_up():
         return pltpu.make_async_remote_copy(
@@ -276,6 +292,17 @@
             field.at[:, pl.ds(first, count), pl.ds(0, ny)], out_ref.at[:, pl.ds(first, count)], local_sem.at[sem]
         )
 
+    def sensitivity_row(x, carry):
+        product_row(steps - 1, x)
+        limit = pltpu.roll(columns[...], nz - cells - x, 1)
+        limit = jnp.broadcast_to(limit[:, 0:1], (ny, nz))
+        inside = lane_index((ny, nz)).astype(jnp.float32) < limit
+        sens = jnp.where(inside, -0.7 * coef[x] * total[x], 0.0)
+        coarse = sens.astype(jnp.bfloat16)
+        sens_ref[x, :, 0:nz] = coarse
+        sens_ref[x, :, nz : 2 * nz] = (sens - coarse.astype(jnp.float32)).astype(jnp.bfloat16)
+        return carry
+
     for s in range(steps):
 
         def inner_curl(x, carry):
@@ -302,49 +329,44 @@
         if s == min(1, steps - 1):
             regularize()
 
-        @pl.when(has_high)
-        def _():
-            copy_up(s).wait_send()
-            copy_down(s).wait_recv()
-
-        @pl.when(has_low)
-        def _():
-            copy_down(s).wait_send()
-            copy_up(s).wait_recv()
-
-        curl_row(cells - 1, lambda at: (from_high[s, 0, at, :], from_high[s, 1, at, :]))
-
-        @pl.when(has_low)
-        def _():
-            for y, size in chunks:
-                at, to = pl.ds(y, size), pl.ds(y + 8, size)
-                curl[1, 0, to, :] = from_low[s, 0, at, :] - field[2, 0, at, :]
-                curl[2, 0, to, :] = from_low[s, 1, at, :] + field[1, 0, at, :]
-
-        @pl.when(jnp.logical_not(has_low))
-        def _():
-            for a in (1, 2):
-                curl[a, 0] = jnp.zeros(curl.shape[2:], jnp.float32)
-
-        update_row(s, cells - 1)
-        if s < steps - 1:
-            send_high(s + 1)
-        update_row(s, 0)
-        if s < steps - 1:
-            send_low(s + 1)
+        if s == steps - 1:
+            load_terms[s].wait()
+            lax.fori_loop(1, cells - 1, sensitivity_row, 0)
+        for part, (first, last) in enumerate(halves(s)):
+            where = pieces(first, last)
+
+            @pl.when(has_high)
+            def _():
+                copy_up(s, part).wait_send()
+                copy_down(s, part).wait_recv()
+
+            curl_row(cells - 1, lambda at: (from_high[s, 0, at, :], from_high[s, 1, at, :]), where)
+            update_row(s, cells - 1, where)
+            if s < steps - 1:
+                send_high(s + 1, part)
+
+            @pl.when(has_low)
+            def _():
+                copy_down(s, part).wait_send()
+                copy_up(s, part).wait_recv()
+                for y, size in where:
+                    at, to = pl.ds(y, size), pl.ds(y + 8, size)
+                    curl[1, 0, to, :] = from_low[s, 0, at, :] - field[2, 0, at, :]
+                    curl[2, 0, to, :] = from_low[s, 1, at, :] + field[1, 0, at, :]
+
+            @pl.when(jnp.logical_not(has_low))
+            def _():
+                for a in (1, 2):
+                    curl[a, 0, pl.ds(first + 8, last - first), :] = jnp.zeros((last - first, nz), jnp.float32)
+
+            update_row(s, 0, where)
+            if s < steps - 1:
+                send_low(s + 1, part)
     store(0, 1, 4).start()
     store(cells - 1, 1, 5).start()
 
-    load_terms[steps - 1].wait()
-    for x in range(cells):
-        product_row(steps - 1, x)
-        inside = lane_index((ny, nz)).astype(jnp.float32) < jnp.broadcast_to(
-            columns[:, cells + x : cells + x + 1], (ny, nz)
-        )
-        sens = jnp.where(inside, -0.7 * coef[x] * total[x], 0.0)
-        coarse = sens.astype(jnp.bfloat16)
-        sens_ref[x, :, 0:nz] = coarse
-        sens_ref[x, :, nz : 2 * nz] = (sens - coarse.astype(jnp.float32)).astype(jnp.bfloat16)
+    sensitivity_row(0, 0)
+    sensitivity_row(cells - 1, 0)
     store(1, cells - 2, 3).wait()
     store(0, 1, 4).wait()
     store(cells - 1, 1, 5).wait()
@@ -385,10 +407,10 @@
             pltpu.VMEM((ny, nz), f32),
             dma((10,)),
             dma((steps,)),
-            dma((steps,)),
-            dma((steps,)),
-            dma((steps,)),
-            dma((steps,)),
+            dma((steps, 2)),
+            dma((steps, 2)),
+            dma((steps, 2)),
+            dma((steps, 2)),
             dma((2,)),
             dma((2,)),
         ],

time: 71.7 us -> 71.2 us (level)
    pallas_call x1, Pallas kernels: 43.4 us -> 42.3 us  [relayout(): pl.pallas_call(functools.partial(relayout_kernel, n), out_shape=jax.Shape...]
where the time goes in v4:
time: 71.2 us; the launch traced here: 71 us
  Pallas kernels  65.7 us (92%)
  local copies, waits for them, and re-layouts  4.61 us (6%)
    pallas_call x1, Pallas kernels, relayout(): pl.pallas_call(functools.partial(relayout_kernel, n), out_shape=jax.Shape...  42.3 us
    pallas_call x1, Pallas kernels, field_phase(): pl.pallas_call(functools.partial(field_kernel, n), out_shape=(jax.ShapeDt...  23.4 us
    unnamed x4, local copies, waits for them, and re-layouts  4.61 us

profile of v4, /device:TPU:0, one launch (start us, length us, event | category | flops | bytes accessed | tf_op | source)
XLA Modules:
  0.0 71.0 jit_solution(12992810318113695084)
XLA Ops:
  0.6 23.4 %shard_map.104 = (f32[3,8,256,128]{3,2,1,0:T(8,128)}, bf16[8,256,256]{2,1,0:T(8,128)(2,1)}, f32[2,256,128]{2,1,0:T(8,128)}) custom-call(f32[3,8,256,128]{3,2,1,0:T(8,128)} %adj_ref.1, bf16[3,3,8,256,128]{4,3,2,1,0:T(8,128)(2,1)} %fwd_ref.1, f32[8,256,128]{2,1,0:T(8,128)} %logc_ref.1, f32[8,256]{1,0:T(8,128)} %spacing_hbm.1, f32[35,8,256]{2,1,0:T(8,128)} %residual_hbm.1, ...), custom_call_target="tpu_custom_call" | custom-call | tf_op jit(solution)/shard_map/pallas_call | solution.py:381
  24.0 42.3 %shard_map.105 = f32[512,128]{1,0:T(8,128)} custom-call(bf16[2048,256]{1,0:T(8,128)(2,1)} %bitcast.3, s32[8,256]{1,0:T(8,128)} %voxel_hbm.1, f32[512,128]{1,0:T(8,128)} %bitcast.5), custom_call_target="tpu_custom_call" | custom-call | tf_op jit(solution)/shard_map/pallas_call | solution.py:606
  66.4 0.0 copy-start
  66.4 3.9 %copy.13 = f32[3,8,256,128]{3,2,1,0:T(8,128)} copy(f32[3,8,256,128]{3,2,1,0:T(8,128)} %get-tuple-element.10) | data formatting | bytes 6291456
  70.3 0.0 copy-done
  70.3 0.7 copy.14
Async XLA Ops:
  66.4 3.9 %copy-start = (f32[512,128]{1,0:T(8,128)S(1)}, f32[512,128]{1,0:T(8,128)}, u32[]{:S(2)}) copy-start(f32[512,128]{1,0:T(8,128)} %shard_map.105) | copy-start | bytes 786436

commit v5 on v4

--- a/solution.py
+++ b/solution.py
@@ -632,6 +632,39 @@
     return out.reshape(regularity.shape)
 
 
+def deliver_kernel(adj_ref, grad_ref, adj_out, grad_out, adj, grad, load_sem, store_sem):
+    cells = adj_ref.shape[1]
+    moves = [(adj_ref.at[:, x], adj.at[:, x], adj_out.at[:, x]) for x in range(cells)]
+    moves.append((grad_ref, grad, grad_out))
+    loads = [pltpu.make_async_copy(a, b, load_sem.at[i]) for i, (a, b, _) in enumerate(moves)]
+    stores = [pltpu.make_async_copy(b, c, store_sem.at[i]) for i, (_, b, c) in enumerate(moves)]
+    for copy in loads:
+        copy.start()
+    for load, copy in zip(loads, stores):
+        load.wait()
+        copy.start()
+    for copy in stores:
+        copy.wait()
+
+
+def deliver(adjoint, gradient):
+    far = pl.BlockSpec(memory_space=pltpu.HBM)
+    copies = adjoint.shape[1] + 1
+    return pl.pallas_call(
+        deliver_kernel,
+        out_shape=tuple(jax.ShapeDtypeStruct(v.shape, v.dtype) for v in (adjoint, gradient)),
+        in_specs=[far, far],
+        out_specs=(far, far),
+        scratch_shapes=[
+            pltpu.VMEM(adjoint.shape, adjoint.dtype),
+            pltpu.VMEM(gradient.shape, gradient.dtype),
+            pltpu.SemaphoreType.DMA((copies,)),
+            pltpu.SemaphoreType.DMA((copies,)),
+        ],
+        compiler_params=pltpu.CompilerParams(vmem_limit_bytes=60 << 20),
+    )(adjoint, gradient)
+
+
 def body(
     adjoint_in,
     forward_terms,
@@ -656,7 +689,7 @@
         voxel_model,
     )
     gradient = relayout(tile_count, sensitivity, voxel_column, regularity)
-    return (adjoint, gradient)
+    return deliver(adjoint, gradient)
 
 
 def solution(mesh):

time: 71.2 us -> 69.5 us (0.976)
  local copies, waits for them, and re-layouts: 4.61 us -> 0 us
  Pallas kernels: 65.7 us -> 68.6 us
    unnamed x4 -> x0, local copies, waits for them, and re-layouts: 4.61 us -> none
    pallas_call x0 -> x1, Pallas kernels: none -> 2.89 us  [deliver(): pl.pallas_call(deliver_kernel, out_shape=tuple((jax.ShapeDtypeStruct(v.sh...]
where the time goes in v5:
time: 69.5 us; the launch traced here: 69.3 us
  Pallas kernels  68.6 us (99%)
    pallas_call x1, Pallas kernels, relayout(): pl.pallas_call(functools.partial(relayout_kernel, n), out_shape=jax.Shape...  42.3 us
    pallas_call x1, Pallas kernels, field_phase(): pl.pallas_call(functools.partial(field_kernel, n), out_shape=(jax.ShapeDt...  23.4 us
    pallas_call x1, Pallas kernels, deliver(): pl.pallas_call(deliver_kernel, out_shape=tuple((jax.ShapeDtypeStruct(v.sh...  2.89 us

profile of v5, /device:TPU:0, one launch (start us, length us, event | category | flops | bytes accessed | tf_op | source)
XLA Modules:
  0.0 69.3 jit_solution(2643647308705077418)
XLA Ops:
  0.6 23.4 %shard_map.104 = (f32[3,8,256,128]{3,2,1,0:T(8,128)}, bf16[8,256,256]{2,1,0:T(8,128)(2,1)}, f32[2,256,128]{2,1,0:T(8,128)}) custom-call(f32[3,8,256,128]{3,2,1,0:T(8,128)} %adj_ref.1, bf16[3,3,8,256,128]{4,3,2,1,0:T(8,128)(2,1)} %fwd_ref.1, f32[8,256,128]{2,1,0:T(8,128)} %logc_ref.1, f32[8,256]{1,0:T(8,128)} %spacing_hbm.1, f32[35,8,256]{2,1,0:T(8,128)} %residual_hbm.1, ...), custom_call_target="tpu_custom_call" | custom-call | tf_op jit(solution)/shard_map/pallas_call | solution.py:381
  24.0 42.3 %shard_map.105 = f32[512,128]{1,0:T(8,128)} custom-call(bf16[2048,256]{1,0:T(8,128)(2,1)} %bitcast.3, s32[8,256]{1,0:T(8,128)} %voxel_hbm.1, f32[512,128]{1,0:T(8,128)} %bitcast.5), custom_call_target="tpu_custom_call" | custom-call | tf_op jit(solution)/shard_map/pallas_call | solution.py:606
  66.4 2.9 %shard_map.106 = (f32[3,8,256,128]{3,2,1,0:T(8,128)}, f32[2,256,128]{2,1,0:T(8,128)}) custom-call(f32[3,8,256,128]{3,2,1,0:T(8,128)} %get-tuple-element.5.adj_ref, f32[2,256,128]{2,1,0:T(8,128)} %bitcast.4), custom_call_target="tpu_custom_call" | custom-call | tf_op jit(solution)/shard_map/pallas_call | solution.py:653

commit v6 on v5

--- a/solution.py
+++ b/solution.py
@@ -454,7 +454,10 @@
         return (z * 2 + y) * 2 + c
 
     def layer_at(k):
-        return up * (layers - 1 - k) + (1 - up) * k
+        above = layers - 1 - layer
+        rising = jnp.where(k < above, layers - 1 - k, k - above)
+        falling = jnp.where(k < layer, k, layers - 1 - (k - layer))
+        return up * rising + (1 - up) * falling
 
     loads = [
         pltpu.make_async_copy(source, target, load_sem.at[i])
@@ -563,7 +566,7 @@
     pair_copy(0, 0).start()
     lax.fori_loop(0, blocks, stage, 0)
     forward(blocks - 1)
-    own = up * (layers - 1 - layer) + (1 - up) * layer
+    own = layers - 1
     for part in range(2):
         at = pl.ds(part * size, size)
         out_ref[at, :] = reg[at, :] + held[2 * own + part]

time: 69.5 us -> 68 us (0.978)
  Pallas kernels: 68.6 us -> 67.2 us
    pallas_call x1, Pallas kernels: 42.3 us -> 40.9 us  [relayout(): pl.pallas_call(functools.partial(relayout_kernel, n), out_shape=jax.Shape...]
where the time goes in v6:
time: 68 us; the launch traced here: 67.8 us
  Pallas kernels  67.2 us (99%)
    pallas_call x1, Pallas kernels, relayout(): pl.pallas_call(functools.partial(relayout_kernel, n), out_shape=jax.Shape...  40.9 us
    pallas_call x1, Pallas kernels, field_phase(): pl.pallas_call(functools.partial(field_kernel, n), out_shape=(jax.ShapeDt...  23.4 us
    pallas_call x1, Pallas kernels, deliver(): pl.pallas_call(deliver_kernel, out_shape=tuple((jax.ShapeDtypeStruct(v.sh...  2.89 us

profile of v6, /device:TPU:0, one launch (start us, length us, event | category | flops | bytes accessed | tf_op | source)
XLA Modules:
  0.0 67.8 jit_solution(15672965907779637266)
XLA Ops:
  0.6 23.4 %shard_map.104 = (f32[3,8,256,128]{3,2,1,0:T(8,128)}, bf16[8,256,256]{2,1,0:T(8,128)(2,1)}, f32[2,256,128]{2,1,0:T(8,128)}) custom-call(f32[3,8,256,128]{3,2,1,0:T(8,128)} %adj_ref.1, bf16[3,3,8,256,128]{4,3,2,1,0:T(8,128)(2,1)} %fwd_ref.1, f32[8,256,128]{2,1,0:T(8,128)} %logc_ref.1, f32[8,256]{1,0:T(8,128)} %spacing_hbm.1, f32[35,8,256]{2,1,0:T(8,128)} %residual_hbm.1, ...), custom_call_target="tpu_custom_call" | custom-call | tf_op jit(solution)/shard_map/pallas_call | solution.py:381
  24.0 40.9 %shard_map.105 = f32[512,128]{1,0:T(8,128)} custom-call(bf16[2048,256]{1,0:T(8,128)(2,1)} %bitcast.3, s32[8,256]{1,0:T(8,128)} %voxel_hbm.1, f32[512,128]{1,0:T(8,128)} %bitcast.5), custom_call_target="tpu_custom_call" | custom-call | tf_op jit(solution)/shard_map/pallas_call | solution.py:609
  64.9 2.9 %shard_map.106 = (f32[3,8,256,128]{3,2,1,0:T(8,128)}, f32[2,256,128]{2,1,0:T(8,128)}) custom-call(f32[3,8,256,128]{3,2,1,0:T(8,128)} %get-tuple-element.5.adj_ref, f32[2,256,128]{2,1,0:T(8,128)} %bitcast.4), custom_call_target="tpu_custom_call" | custom-call | tf_op jit(solution)/shard_map/pallas_call | solution.py:656
